TPU v7x, 32 devices: a whole 2x2x4 slice. The times are simulated.
32 devices in a mesh: dp: 16 (over z, y, x), zero: 2 (over core).
Axes of the slice: x: 2, y: 2, z: 4, core: 2. Of those that a mesh axis runs over, the one named last changes fastest.
Arguments:
- tokens: bfloat16 [8192, 768], P(('dp', 'zero')), may hold values from -6 to 6
- cotangent: bfloat16 [8192, 768], P(('dp', 'zero')), may hold values from -6 to 6
- segment_ids: int32 [32, 256], P(('dp', 'zero')), may hold values from 0 to 5, never falling along the last dimension, each value on 1 to 128 neighbouring positions
- packed_weights: float32 [768, 6144], P(None, ('dp', 'zero')), may hold values from -0.5412659 to 0.5412659
- down_weights: float32 [3072, 768], P(('dp', 'zero')), may hold values from -0.109375 to 0.109375
- vector_params: float32 [13, 768], P(None, 'zero'), may hold values from -1.5 to 3.5, as said below
- packed_first: float32 [768, 6144], P(None, ('dp', 'zero')), may hold values from -6.788225 to 6.788225
- packed_second: float32 [768, 6144], P(None, ('dp', 'zero')), may hold values from 0.32768 to 66.3552
- down_first: float32 [3072, 768], P(('dp', 'zero')), may hold values from -16 to 16
- down_second: float32 [3072, 768], P(('dp', 'zero')), may hold values from 16.384 to 163.84
- vector_first: float32 [13, 768], P(None, 'zero'), may hold values from -28 to 28
- vector_second: float32 [13, 768], P(None, 'zero'), may hold values from 40.96 to 409.6
Outputs:
- block_output: bfloat16 [8192, 768], P(('dp', 'zero'))
- tokens_grad: float32 [8192, 768], P(('dp', 'zero'))
- packed_grad: float32 [768, 6144], P(None, ('dp', 'zero'))
- down_grad: float32 [3072, 768], P(('dp', 'zero'))
- vector_grad: float32 [13, 768], P(None, 'zero')
- packed_new: float32 [768, 6144], P(None, ('dp', 'zero'))
- down_new: float32 [3072, 768], P(('dp', 'zero'))
- vector_step: float32 [13, 768], P(None, 'zero')
- packed_first_new: float32 [768, 6144], P(None, ('dp', 'zero'))
- packed_second_new: float32 [768, 6144], P(None, ('dp', 'zero'))
- down_first_new: float32 [3072, 768], P(('dp', 'zero'))
- down_second_new: float32 [3072, 768], P(('dp', 'zero'))
- vector_first_new: float32 [13, 768], P(None, 'zero')
- vector_second_new: float32 [13, 768], P(None, 'zero')
Inputs may be any that keep to these rules, and one draw needn't show every extreme that they name: `segment_ids`: each row holds 6 sequences numbered in order, each of 1 to 128 slots, one of exactly 128. `vector_params`: rows 0 and 2 are positive.
All inputs are finite; a program needn't handle non-finite values.
Results may differ from a plain program's by a relative error of at most 0.0025.
The roundings to bfloat16 on the way count: a program that leaves them out, or rounds other values in their place, can miss the bound.
Values may be sent and summed in bfloat16 or wider, within the bound.
A program may use at most 192 MiB of HBM per device.

v0:
```python
import jax
import jax.numpy as jnp
from jax import lax
from jax.sharding import PartitionSpec as P

H = 12
HEAD = 64
ROT = 16
STEP_COUNT = 4


norm_epsilon = 1e-05
adam_epsilon = 1e-08
learn_rate = 0.01
decay_rate = 0.1
beta_first = 0.9
beta_second = 0.95
rope_base = 10000.0
masked_value = -1e30
inv_sqrt_two = 0.7071067811865476
inv_sqrt_tau = 0.3989422804014327


def contract(form, left, right):
    return jnp.einsum(form, left, right, preferred_element_type=jnp.float32)


def layer_norm(residual, gain_vector, bias_vector):
    centered = residual - jnp.mean(residual, axis=-1, keepdims=True)
    inverse = lax.rsqrt(jnp.mean(centered * centered, axis=-1, keepdims=True) + norm_epsilon)
    normalized = centered * inverse
    return (normalized * gain_vector + bias_vector, normalized, inverse)


def norm_backward(grad_normed, normalized, inverse, gain_vector):
    grad_gain = jnp.sum(grad_normed * normalized, axis=0)
    grad_bias = jnp.sum(grad_normed, axis=0)
    grad_hat = grad_normed * gain_vector
    grad_input = inverse * (
        grad_hat
        - jnp.mean(grad_hat, axis=-1, keepdims=True)
        - normalized * jnp.mean(grad_hat * normalized, axis=-1, keepdims=True)
    )
    return (grad_input, grad_gain, grad_bias)


def rotary_tables(segment_row):
    row_count = segment_row.shape[0]
    positions_all = jnp.arange(row_count, dtype=jnp.int32)
    same_segment = segment_row[:, None] == segment_row[None, :]
    starts = jnp.min(jnp.where(same_segment, positions_all[None, :], row_count), axis=1)
    offsets = (positions_all - starts).astype(jnp.float32)
    half_rot = ROT // 2
    frequency = jnp.power(rope_base, -(jnp.arange(half_rot, dtype=jnp.float32) * 2.0 / ROT))
    angles = offsets[:, None] * frequency[None, :]
    allowed = same_segment & (positions_all[None, :] <= positions_all[:, None])
    return (jnp.cos(angles)[:, None, :], jnp.sin(angles)[:, None, :], allowed)


def rotate_heads(values, cosine, sine_table):
    half_rot = ROT // 2
    front = values[..., :half_rot]
    behind = values[..., half_rot:ROT]
    return jnp.concatenate(
        [
            front * cosine - behind * sine_table,
            behind * cosine + front * sine_table,
            values[..., ROT:],
        ],
        axis=-1,
    )


def gelu_parts(upward):
    normal_cdf = 0.5 * (1.0 + lax.erf(upward * inv_sqrt_two))
    density = jnp.exp(-0.5 * upward * upward) * inv_sqrt_tau
    return (upward * normal_cdf, normal_cdf + upward * density)


def layer_rows(token_rows, cotangent_rows, segment_row, packed_low, down_low, vector_low):
    row_count, model_width = token_rows.shape
    ffn_width = down_low.shape[0]
    vector_full = vector_low.astype(jnp.float32)
    residual = token_rows.astype(jnp.float32)
    normed_one, unit_one, inverse_one = layer_norm(residual, vector_full[0], vector_full[1])
    normed_two, unit_two, inverse_two = layer_norm(residual, vector_full[2], vector_full[3])
    normed_one_low = normed_one.astype(jnp.bfloat16)
    normed_two_low = normed_two.astype(jnp.bfloat16)
    weight_qkv = packed_low[:, : 3 * model_width]
    weight_out = packed_low[:, 3 * model_width : 4 * model_width]
    weight_up = packed_low[:, 4 * model_width :]
    bias_qkv = vector_full[6:9].reshape(3 * model_width)
    bias_up = vector_full[9:].reshape(ffn_width)
    projected = jnp.dot(normed_one_low, weight_qkv, preferred_element_type=jnp.float32) + bias_qkv
    heads_shape = (row_count, H, HEAD)
    cosine, sine_table, allowed = rotary_tables(segment_row)
    query_low = rotate_heads(
        projected[:, :model_width].reshape(heads_shape), cosine, sine_table
    ).astype(jnp.bfloat16)
    key_low = rotate_heads(
        projected[:, model_width : 2 * model_width].reshape(heads_shape), cosine, sine_table
    ).astype(jnp.bfloat16)
    value_low = projected[:, 2 * model_width :].reshape(heads_shape).astype(jnp.bfloat16)
    score_scale = HEAD ** (-0.5)

    def attention_scores():
        scores = contract("qhd,khd->hqk", query_low, key_low) * score_scale
        return jnp.where(allowed[None], scores, masked_value)

    scores = attention_scores()
    log_total = jnp.log(jnp.sum(jnp.exp(scores), axis=-1, keepdims=True))
    probs_low = jnp.exp(scores - log_total).astype(jnp.bfloat16)
    attended = contract("hqk,khd->qhd", probs_low, value_low)
    attended_low = attended.reshape(row_count, model_width).astype(jnp.bfloat16)
    branch_attn = (
        jnp.dot(attended_low, weight_out, preferred_element_type=jnp.float32) + vector_full[4]
    )
    upward = jnp.dot(normed_two_low, weight_up, preferred_element_type=jnp.float32) + bias_up
    activated, gelu_slope = gelu_parts(upward)
    activated_low = activated.astype(jnp.bfloat16)
    branch_mlp = (
        jnp.dot(activated_low, down_low, preferred_element_type=jnp.float32) + vector_full[5]
    )
    block_output = (residual + branch_attn + branch_mlp).astype(jnp.bfloat16)
    grad_rows = cotangent_rows.astype(jnp.float32)
    grad_bias_rows = jnp.sum(grad_rows, axis=0)
    grad_down = jnp.dot(activated_low.T, cotangent_rows, preferred_element_type=jnp.float32)
    grad_upward = (
        jnp.dot(cotangent_rows, down_low.T, preferred_element_type=jnp.float32) * gelu_slope
    )
    grad_upward_low = grad_upward.astype(jnp.bfloat16)
    grad_weight_up = jnp.dot(normed_two_low.T, grad_upward_low, preferred_element_type=jnp.float32)
    grad_normed_two = jnp.dot(grad_upward_low, weight_up.T, preferred_element_type=jnp.float32)
    grad_weight_out = jnp.dot(attended_low.T, cotangent_rows, preferred_element_type=jnp.float32)
    grad_attended_low = (
        jnp.dot(cotangent_rows, weight_out.T, preferred_element_type=jnp.float32)
        .astype(jnp.bfloat16)
        .reshape(heads_shape)
    )
    correction = jnp.sum(grad_attended_low.astype(jnp.float32) * attended, axis=-1)
    attention_probs = jnp.exp(attention_scores() - log_total)
    grad_probs = contract("qhd,khd->hqk", grad_attended_low, value_low)
    grad_scores_low = (
        attention_probs * (grad_probs - correction.T[:, :, None]) * score_scale
    ).astype(jnp.bfloat16)
    probs_again = attention_probs.astype(jnp.bfloat16)
    grad_query = contract("hqk,khd->qhd", grad_scores_low, key_low)
    grad_key = contract("hqk,qhd->khd", grad_scores_low, query_low)
    grad_value = contract("hqk,qhd->khd", probs_again, grad_attended_low)
    grad_projected = jnp.concatenate(
        [
            rotate_heads(grad_query, cosine, -sine_table).reshape(row_count, model_width),
            rotate_heads(grad_key, cosine, -sine_table).reshape(row_count, model_width),
            grad_value.reshape(row_count, model_width),
        ],
        axis=1,
    )
    grad_projected_low = grad_projected.astype(jnp.bfloat16)
    grad_weight_qkv = jnp.dot(
        normed_one_low.T, grad_projected_low, preferred_element_type=jnp.float32
    )
    grad_normed_one = jnp.dot(grad_projected_low, weight_qkv.T, preferred_element_type=jnp.float32)
    input_one, gain_one, bias_one = norm_backward(
        grad_normed_one, unit_one, inverse_one, vector_full[0]
    )
    input_two, gain_two, bias_two = norm_backward(
        grad_normed_two, unit_two, inverse_two, vector_full[2]
    )
    grad_tokens = grad_rows + input_one + input_two
    grad_packed = jnp.concatenate([grad_weight_qkv, grad_weight_out, grad_weight_up], axis=1)
    grad_vector = jnp.concatenate(
        [
            jnp.stack([gain_one, bias_one, gain_two, bias_two, grad_bias_rows, grad_bias_rows]),
            jnp.sum(grad_projected, axis=0).reshape(3, model_width),
            jnp.sum(grad_upward, axis=0).reshape(ffn_width // model_width, model_width),
        ],
        axis=0,
    )
    return (block_output, grad_tokens, grad_packed, grad_down, grad_vector)


def adam_moments(first_moment, second, grad_total):
    first_new = beta_first * first_moment + (1.0 - beta_first) * grad_total
    second_new = beta_second * second + (1.0 - beta_second) * grad_total * grad_total
    first_hat = first_new / (1.0 - beta_first**STEP_COUNT)
    second_hat = second_new / (1.0 - beta_second**STEP_COUNT)
    return (first_new, second_new, first_hat / (jnp.sqrt(second_hat) + adam_epsilon))


def adam_update(weight, first_moment, second, grad_total):
    first_new, second_new, direction = adam_moments(first_moment, second, grad_total)
    weight_new = weight * (1.0 - learn_rate * decay_rate) - learn_rate * direction
    return (weight_new, first_new, second_new)


def adam_change(weight, first_moment, second, grad_total):
    first_new, second_new, direction = adam_moments(first_moment, second, grad_total)
    change = -(learn_rate * decay_rate) * weight - learn_rate * direction
    return (change, first_new, second_new)


def body(
    tokens,
    cotangent,
    segment_ids,
    packed_weights,
    down_weights,
    vector_params,
    packed_first,
    packed_second,
    down_first,
    down_second,
    vector_first,
    vector_second,
):
    packed_shard = packed_weights.astype(jnp.bfloat16)
    down_shard = down_weights.astype(jnp.bfloat16)
    vector_shard = vector_params.astype(jnp.bfloat16)
    packed_full, down_full = (
        lax.all_gather(packed_shard, ("dp", "zero"), axis=1, tiled=True),
        lax.all_gather(down_shard, ("dp", "zero"), axis=0, tiled=True),
    )
    vector_full = lax.all_gather(vector_shard, "zero", axis=1, tiled=True)
    block_output, grad_tokens, grad_packed, grad_down, grad_vector = layer_rows(
        tokens, cotangent, segment_ids[0], packed_full, down_full, vector_full
    )
    packed_sum, down_sum = (
        lax.psum_scatter(grad_packed, ("dp", "zero"), scatter_dimension=1, tiled=True),
        lax.psum_scatter(grad_down, ("dp", "zero"), scatter_dimension=0, tiled=True),
    )
    vector_part = lax.psum_scatter(grad_vector, "zero", scatter_dimension=1, tiled=True)
    vector_sum = lax.psum(vector_part, "dp")
    packed_new, packed_first_new, packed_second_new = adam_update(
        packed_weights, packed_first, packed_second, packed_sum
    )
    down_new, down_first_new, down_second_new = adam_update(
        down_weights, down_first, down_second, down_sum
    )
    vector_step, vector_first_new, vector_second_new = adam_change(
        vector_params, vector_first, vector_second, vector_sum
    )
    return (
        block_output,
        grad_tokens,
        packed_sum,
        down_sum,
        vector_sum,
        packed_new,
        down_new,
        vector_step,
        packed_first_new,
        packed_second_new,
        down_first_new,
        down_second_new,
        vector_first_new,
        vector_second_new,
    )


def solution(mesh):
    return jax.shard_map(
        body,
        mesh=mesh,
        in_specs=(
            P(("dp", "zero"), None),
            P(("dp", "zero"), None),
            P(("dp", "zero"), None),
            P(None, ("dp", "zero")),
            P(("dp", "zero"), None),
            P(None, "zero"),
            P(None, ("dp", "zero")),
            P(None, ("dp", "zero")),
            P(("dp", "zero"), None),
            P(("dp", "zero"), None),
            P(None, "zero"),
            P(None, "zero"),
        ),
        out_specs=(
            P(("dp", "zero"), None),
            P(("dp", "zero"), None),
            P(None, ("dp", "zero")),
            P(("dp", "zero"), None),
            P(None, "zero"),
            P(None, ("dp", "zero")),
            P(("dp", "zero"), None),
            P(None, "zero"),
            P(None, ("dp", "zero")),
            P(None, ("dp", "zero")),
            P(("dp", "zero"), None),
            P(("dp", "zero"), None),
            P(None, "zero"),
            P(None, "zero"),
        ),
        check_vma=False,
    )
```

profile of v0, /device:TPU:0, one launch (start us, length us, event | category | flops | bytes accessed | tf_op | source)
XLA Modules:
  0.0 583.2 jit_solution(729901724365719443)
XLA Ops:
  14.8 81.4 %all-gather.3.cloned.1.call-done = bf16[768,6144]{0,1:T(8,128)(2,1)} async-done(((bf16[768,192]{0,1:T(8,128)(2,1)}), bf16[768,6144]{0,1:T(8,128)(2,1)}) %all-gather.3.cloned.1.call-update) | async-done | bytes 9437200 | tf_op jit(solution)/shard_map/all_gather | solution.py:220
  96.3 5.7 multiply_convert_fusion.1
  103.1 5.1 fusion.102
  108.3 134.0 %reduce-scatter.6.cloned.1.call-done = f32[96,768]{1,0:T(8,128)} async-done(((f32[3072,768]{1,0:T(8,128)}), f32[96,768]{1,0:T(8,128)}) %reduce-scatter.6.cloned.1.call-update) | async-done | bytes 294928 | tf_op jit(solution)/shard_map/reduce_scatter | solution.py:229
  249.0 3.2 convolution_add_fusion
  259.7 4.9 multiply_reduce_fusion
  264.5 4.8 fusion.12
  269.3 3.0 multiply_convert_fusion
  274.9 4.7 fusion.57
  282.4 4.8 fusion.87
  287.2 21.4 %all-gather.5.cloned.1.call-done = bf16[3072,768]{1,0:T(8,128)(2,1)} async-done(((bf16[96,768]{1,0:T(8,128)(2,1)}), bf16[3072,768]{1,0:T(8,128)(2,1)}) %all-gather.5.cloned.1.call-update) | async-done | bytes 4718608 | tf_op jit(solution)/shard_map/all_gather | solution.py:221
  308.6 6.3 %fusion.100 = (f32[3072]{0:T(1024)}, bf16[256,3072]{1,0:T(8,128)(2,1)S(1)}) fusion(f32[256,3072]{1,0:T(8,128)} %get-tuple-element.106, bf16[256,768]{1,0:T(8,128)(2,1)} %param.13, bf16[3072,768]{1,0:T(8,128)(2,1)} %all-gather.5.cloned.1.call-done), kind=kOutput, calls=%fused_computation.139 | convolution fusion | flops 1216607232 | bytes 9842688 | tf_op jit(solution)/shard_map/dot_general | solution.py:129
  314.8 5.2 fusion.54
  324.6 3.4 concatenate.29
  328.1 13.6 %pad_maximum_fusion = f32[768,6144]{1,0:T(8,128)} fusion(f32[768,3072]{1,0:T(8,128)} %fusion.54, f32[768,768]{1,0:T(8,128)S(1)} %fusion.101, f32[768,2304]{1,0:T(8,128)} %fusion.87), kind=kLoop, calls=%fused_computation.1 | loop fusion | flops 9437184 | bytes 37748736 | tf_op jit(solution)/shard_map/concatenate | solution.py:170
  341.8 18.7 %copy.88 = f32[768,6144]{0,1:T(8,128)} copy(f32[768,6144]{1,0:T(8,128)} %pad_maximum_fusion) | data formatting | bytes 37748736
  362.9 4.6 convolution_add_fusion.2
  367.6 2.7 fusion.26
  370.3 75.8 %psum.7 = f32[13,384]{1,0:T(8,128)S(1)} all-reduce(f32[13,384]{1,0:T(8,128)} %reduce-scatter.8.cloned.1.call-done), channel_id=1, replica_groups=mesh['dp'=16,'zero'=2] {'dp'}, use_global_device_ids=true, to_apply=%region_19.20 | all-reduce | flops 4992 | bytes 39936 | tf_op jit(solution)/shard_map/psum | solution.py:232
  446.7 119.4 %reduce-scatter.10.cloned.1.call-done = f32[192,768]{1,0:T(8,128)} async-done(((f32[6144,768]{1,0:T(8,128)}), f32[192,768]{1,0:T(8,128)}) %reduce-scatter.10.cloned.1.call-update) | async-done | bytes 589840
  566.1 2.2 copy.89
  568.4 2.8 multiply_subtract_fusion
  571.2 2.2 copy.79
  573.4 2.2 copy.80
  (169 shorter events, 36.6 us)
Async XLA Ops:
  7.2 89.1 %all-gather.3.cloned.1.call-start = ((), (), s32[]{:S(2)}) async-start(), calls=%async_computation.3 | async-start | bytes 9732096 | tf_op jit(solution)/shard_map/all_gather | solution.py:220
  9.1 233.3 %reduce-scatter.6.cloned.1.call-start = ((), (), s32[]{:S(2)}) async-start(), calls=%async_computation.5 | async-start | bytes 9732096 | tf_op jit(solution)/shard_map/reduce_scatter | solution.py:229
  13.6 235.4 %copy-start.35 = (f32[256]{0:T(256)}, f32[256]{0:T(256)S(1)}, u32[]{:S(2)}) copy-start(f32[256]{0:T(256)S(1)} %broadcast_multiply_fusion.4) | copy-start | bytes 3076
  14.8 234.1 %copy-start.38 = (f32[256]{0:T(256)}, f32[256]{0:T(256)S(1)}, u32[]{:S(2)}) copy-start(f32[256]{0:T(256)S(1)} %add_rsqrt_fusion) | copy-start | bytes 3076
  96.3 6.9 %copy-start.4 = (bf16[256,768]{1,0:T(8,128)(2,1)S(1)}, bf16[256,768]{1,0:T(8,128)(2,1)}, u32[]{:S(2)}) copy-start(bf16[256,768]{1,0:T(8,128)(2,1)} %param.13) | copy-start | bytes 1179652
  108.2 134.1 %copy-start.28 = (f32[96,768]{1,0:T(8,128)S(1)}, f32[96,768]{1,0:T(8,128)}, u32[]{:S(2)}) copy-start(f32[96,768]{1,0:T(8,128)} %param.16) | copy-start | bytes 884740
  108.2 134.1 %copy-start.29 = (f32[96,768]{1,0:T(8,128)S(1)}, f32[96,768]{1,0:T(8,128)}, u32[]{:S(2)}) copy-start(f32[96,768]{1,0:T(8,128)} %param.20) | copy-start | bytes 884740
  108.2 134.1 %copy-start.30 = (f32[96,768]{1,0:T(8,128)S(1)}, f32[96,768]{1,0:T(8,128)}, u32[]{:S(2)}) copy-start(f32[96,768]{1,0:T(8,128)} %param.21) | copy-start | bytes 884740
  108.2 136.5 %copy-start.43 = (s32[1,256]{1,0:T(1,128)S(1)}, s32[1,256]{1,0:T(1,128)}, u32[]{:S(2)}) copy-start(s32[1,256]{1,0:T(1,128)} %param.14) | copy-start | bytes 3076
  108.2 140.7 %copy-start = (bf16[256,768]{1,0:T(8,128)(2,1)S(1)}, bf16[256,768]{1,0:T(8,128)(2,1)}, u32[]{:S(2)}) copy-start(bf16[256,768]{1,0:T(8,128)(2,1)} %param.12) | copy-start | bytes 1179652
  108.2 200.3 %all-gather.5.cloned.1.call-start = ((), (), s32[]{:S(2)}) async-start(), calls=%async_computation.4 | async-start | bytes 4866048 | tf_op jit(solution)/shard_map/all_gather | solution.py:221
  244.4 125.9 %reduce-scatter.8.cloned.1.call-start = ((), (), s32[]{:S(2)}) async-start(), calls=%async_computation.6 | async-start | bytes 73728 | tf_op jit(solution)/shard_map/reduce_scatter | solution.py:231
  245.5 11.8 %copy-start.33 = (f32[256,8]{0,1:T(8,128)}, f32[256,8]{0,1:T(8,128)S(1)}, u32[]{:S(2)}) copy-start(f32[256,8]{0,1:T(8,128)S(1)} %get-tuple-element.104) | copy-start | bytes 24580
  274.9 5.1 copy-start.1
  308.6 6.3 %copy-start.36 = (f32[256]{0:T(256)S(1)}, f32[256]{0:T(256)}, u32[]{:S(2)}) copy-start(f32[256]{0:T(256)} %copy-done.35) | copy-start | bytes 3076
  308.6 6.3 %copy-start.39 = (f32[256]{0:T(256)S(1)}, f32[256]{0:T(256)}, u32[]{:S(2)}) copy-start(f32[256]{0:T(256)} %copy-done.38) | copy-start | bytes 3076
  308.6 11.5 %slice-start = ((s8[9437184]{0:T(1024)(128)(4,1)}), s8[4194304]{0:T(1024)(128)(4,1)S(1)}, s32[]{:S(2)}) async-start(s8[9437184]{0:T(1024)(128)(4,1)} %bitcast.64), calls=%async_computation.8 | async-start | bytes 8388608
  308.6 11.5 %slice-start.1 = ((s8[9437184]{0:T(1024)(128)(4,1)}), s8[4194304]{0:T(1024)(128)(4,1)S(1)}, s32[]{:S(2)}) async-start(s8[9437184]{0:T(1024)(128)(4,1)} %bitcast.64), calls=%async_computation.9 | async-start | bytes 8388608
  314.8 5.2 slice-start.2
  328.1 238.0 %reduce-scatter.10.cloned.1.call-start = ((), (), s32[]{:S(2)}) async-start(), calls=%async_computation.7 | async-start | bytes 19464192
  367.6 78.5 %copy-start.31 = (f32[13,384]{1,0:T(8,128)S(1)}, f32[13,384]{1,0:T(8,128)}, u32[]{:S(2)}) copy-start(f32[13,384]{1,0:T(8,128)} %param.17) | copy-start | bytes 59908
  367.6 78.5 %copy-start.41 = (f32[13,384]{1,0:T(8,128)S(1)}, f32[13,384]{1,0:T(8,128)}, u32[]{:S(2)}) copy-start(f32[13,384]{1,0:T(8,128)} %param.22) | copy-start | bytes 59908
  367.6 78.5 %copy-start.42 = (f32[13,384]{1,0:T(8,128)S(1)}, f32[13,384]{1,0:T(8,128)}, u32[]{:S(2)}) copy-start(f32[13,384]{1,0:T(8,128)} %param.23) | copy-start | bytes 59908
  446.1 125.2 %copy-start.32 = (f32[13,384]{1,0:T(8,128)}, f32[13,384]{1,0:T(8,128)S(1)}, u32[]{:S(2)}) copy-start(f32[13,384]{1,0:T(8,128)S(1)} %psum.7) | copy-start | bytes 59908
  (31 other events, 58.7 us)
Sparse Core Ops, SparseCore 0:
  11.5 84.7 all-gather.2
  108.3 133.9 reduce-scatter.5
  245.6 62.8 all-gather.4
  328.2 6.2 reduce-scatter.7
  360.6 205.4 reduce-scatter.9
where the time goes:
time: 585 us; the launch traced here: 583 us
  waiting for transfers between devices  356 us (61%)
  blocking collectives  77.7 us (13%)
  matrix products  63.9 us (11%)
  local copies, waits for them, and re-layouts  42.8 us (7%)
  other arithmetic  27.7 us (5%)
  between operations  14.5 us (2%)
    reduce_scatter x1, waiting for transfers between devices, body(): lax.psum_scatter(grad_down, ('dp', 'zero'), scatter_dimension=0, tiled=True)  134 us
    unnamed x6, waiting for transfers between devices  119 us
    all_gather x1, waiting for transfers between devices, body(): lax.all_gather(packed_shard, ('dp', 'zero'), axis=1, tiled=True)  81.4 us
    psum x1, blocking collectives, body(): vector_sum = lax.psum(vector_part, 'dp')  75.8 us
    unnamed x108, local copies, waits for them, and re-layouts  33.3 us
    all_gather x1, waiting for transfers between devices, body(): lax.all_gather(down_shard, ('dp', 'zero'), axis=0, tiled=True)  21.4 us
    dot_general x6, matrix products, contract(): return jnp.einsum(form, left, right, preferred_element_type=jnp.float32)  15.1 us
    concatenate x1, other arithmetic, layer_rows(): jnp.concatenate([grad_weight_qkv, grad_weight_out, grad_weight_up], axis=1)  13.6 us
  transfers between devices with their start and end apart: 5, of which 4 were waited for; matrix products, arithmetic and copies ran while one was open for 14% of the time, Pallas kernels for 0%

commit v1 on v0

--- a/solution.py
+++ b/solution.py
@@ -1,3 +1,5 @@
+import functools
+
 import jax
 import jax.numpy as jnp
 from jax import lax
@@ -86,9 +88,9 @@
     normed_two, unit_two, inverse_two = layer_norm(residual, vector_full[2], vector_full[3])
     normed_one_low = normed_one.astype(jnp.bfloat16)
     normed_two_low = normed_two.astype(jnp.bfloat16)
-    weight_qkv = packed_low[:, : 3 * model_width]
-    weight_out = packed_low[:, 3 * model_width : 4 * model_width]
-    weight_up = packed_low[:, 4 * model_width :]
+    weight_qkv = packed_low[: 3 * model_width].T
+    weight_out = packed_low[3 * model_width : 4 * model_width].T
+    weight_up = packed_low[4 * model_width :].T
     bias_qkv = vector_full[6:9].reshape(3 * model_width)
     bias_up = vector_full[9:].reshape(ffn_width)
     projected = jnp.dot(normed_one_low, weight_qkv, preferred_element_type=jnp.float32) + bias_qkv
@@ -129,9 +131,9 @@
         jnp.dot(cotangent_rows, down_low.T, preferred_element_type=jnp.float32) * gelu_slope
     )
     grad_upward_low = grad_upward.astype(jnp.bfloat16)
-    grad_weight_up = jnp.dot(normed_two_low.T, grad_upward_low, preferred_element_type=jnp.float32)
+    grad_weight_up = jnp.dot(grad_upward_low.T, normed_two_low, preferred_element_type=jnp.float32)
     grad_normed_two = jnp.dot(grad_upward_low, weight_up.T, preferred_element_type=jnp.float32)
-    grad_weight_out = jnp.dot(attended_low.T, cotangent_rows, preferred_element_type=jnp.float32)
+    grad_weight_out = jnp.dot(cotangent_rows.T, attended_low, preferred_element_type=jnp.float32)
     grad_attended_low = (
         jnp.dot(cotangent_rows, weight_out.T, preferred_element_type=jnp.float32)
         .astype(jnp.bfloat16)
@@ -157,7 +159,7 @@
     )
     grad_projected_low = grad_projected.astype(jnp.bfloat16)
     grad_weight_qkv = jnp.dot(
-        normed_one_low.T, grad_projected_low, preferred_element_type=jnp.float32
+        grad_projected_low.T, normed_one_low, preferred_element_type=jnp.float32
     )
     grad_normed_one = jnp.dot(grad_projected_low, weight_qkv.T, preferred_element_type=jnp.float32)
     input_one, gain_one, bias_one = norm_backward(
@@ -167,7 +169,7 @@
         grad_normed_two, unit_two, inverse_two, vector_full[2]
     )
     grad_tokens = grad_rows + input_one + input_two
-    grad_packed = jnp.concatenate([grad_weight_qkv, grad_weight_out, grad_weight_up], axis=1)
+    grad_packed = [grad_weight_qkv, grad_weight_out, grad_weight_up]
     grad_vector = jnp.concatenate(
         [
             jnp.stack([gain_one, bias_one, gain_two, bias_two, grad_bias_rows, grad_bias_rows]),
@@ -199,7 +201,97 @@
     return (change, first_new, second_new)
 
 
+AXES = ("dp", "zero")
+
+
+def exchange(value, size, mask):
+    return lax.ppermute(value, AXES, [(i, i ^ mask) for i in range(size)])
+
+
+def stage_lists(bit_count):
+    rest = [(3, 4)] if bit_count >= 5 else [(b,) for b in range(3, bit_count)]
+    rest = rest + [(b,) for b in range(5, bit_count)]
+    return [[(1,), (2,)] + rest, [(2,), (1,)] + rest]
+
+
+def scatter_stage(value, present, group, me, size, wire):
+    span = 1 << len(group)
+    low = group[0]
+    mine = (me >> low) & (span - 1)
+    top = group[-1]
+    axis = present.index(top)
+    shape = value.shape
+    value = value.reshape(shape[:axis] + (span,) + shape[axis + len(group) :])
+    total = lax.dynamic_index_in_dim(value, mine, axis, keepdims=False)
+    for k in range(1, span):
+        part = lax.dynamic_index_in_dim(value, mine ^ k, axis, keepdims=False).astype(wire)
+        total = total + exchange(part, size, k << low).astype(jnp.float32)
+    return total, [b for b in present if b not in group]
+
+
+def scatter_parts(parts, me, size):
+    rows = sum(p.shape[0] for p in parts) // size
+    width = parts[0].shape[1]
+    bit_count = size.bit_length() - 1
+    core = me & 1
+    split = [p.reshape(p.shape[0] // (2 * rows), 2, rows, width) for p in parts]
+    pieces = []
+    half = width // 2
+    for index, stages in enumerate(stage_lists(bit_count)):
+        cut = [p[..., index * half : (index + 1) * half] for p in split]
+        send = jnp.concatenate(
+            [lax.dynamic_index_in_dim(p, 1 - core, 1, keepdims=False) for p in cut], axis=0
+        )
+        keep = jnp.concatenate(
+            [lax.dynamic_index_in_dim(p, core, 1, keepdims=False) for p in cut], axis=0
+        )
+        value = keep + exchange(send, size, 1)
+        present = list(range(bit_count - 1, 0, -1))
+        value = value.reshape((2,) * (bit_count - 1) + (rows, half))
+        for group in stages:
+            wire = jnp.bfloat16 if group in ((1,), (2,)) else jnp.float32
+            value, present = scatter_stage(value, present, group, me, size, wire)
+        pieces.append(value)
+    return jnp.concatenate(pieces, axis=-1)
+
+
+def gather_rows(shard, me, size):
+    rows, width = shard.shape
+    bit_count = size.bit_length() - 1
+    half = width // 2
+    pieces = []
+    for index, stages in enumerate(stage_lists(bit_count)):
+        value = shard[:, index * half : (index + 1) * half]
+        present = []
+        for group in list(reversed(stages)) + [(0,)]:
+            span = 1 << len(group)
+            low = group[0]
+            slots = [value] + [exchange(value, size, k << low) for k in range(1, span)]
+            for t, b in enumerate(group):
+                bit = ((me >> b) & 1) == 1
+                slots = [jnp.where(bit, slots[j ^ (1 << t)], slots[j]) for j in range(span)]
+            axis = sum(1 for b in present if b > group[-1])
+            value = jnp.stack(slots, axis=axis)
+            value = value.reshape(
+                value.shape[:axis] + (2,) * len(group) + value.shape[axis + 1 :]
+            )
+            present = sorted(present + list(group), reverse=True)
+        pieces.append(value.reshape(size * rows, half))
+    return jnp.concatenate(pieces, axis=-1)
+
+
+def reduce_vector(grad_vector, me, size, zero_size):
+    bit_count = size.bit_length() - 1
+    total = grad_vector
+    for b in range(bit_count):
+        total = total + exchange(total, size, 1 << b)
+    width = grad_vector.shape[1] // zero_size
+    return lax.dynamic_slice_in_dim(total, (me % zero_size) * width, width, axis=1)
+
+
 def body(
+    zero_size,
+    size,
     tokens,
     cotangent,
     segment_ids,
@@ -213,23 +305,19 @@
     vector_first,
     vector_second,
 ):
-    packed_shard = packed_weights.astype(jnp.bfloat16)
+    me = lax.axis_index("dp") * zero_size + lax.axis_index("zero")
+    packed_shard = packed_weights.astype(jnp.bfloat16).T
     down_shard = down_weights.astype(jnp.bfloat16)
     vector_shard = vector_params.astype(jnp.bfloat16)
-    packed_full, down_full = (
-        lax.all_gather(packed_shard, ("dp", "zero"), axis=1, tiled=True),
-        lax.all_gather(down_shard, ("dp", "zero"), axis=0, tiled=True),
-    )
+    packed_full = gather_rows(packed_shard, me, size)
+    down_full = gather_rows(down_shard, me, size)
     vector_full = lax.all_gather(vector_shard, "zero", axis=1, tiled=True)
     block_output, grad_tokens, grad_packed, grad_down, grad_vector = layer_rows(
         tokens, cotangent, segment_ids[0], packed_full, down_full, vector_full
     )
-    packed_sum, down_sum = (
-        lax.psum_scatter(grad_packed, ("dp", "zero"), scatter_dimension=1, tiled=True),
-        lax.psum_scatter(grad_down, ("dp", "zero"), scatter_dimension=0, tiled=True),
-    )
-    vector_part = lax.psum_scatter(grad_vector, "zero", scatter_dimension=1, tiled=True)
-    vector_sum = lax.psum(vector_part, "dp")
+    down_sum = scatter_parts([grad_down], me, size)
+    packed_sum = scatter_parts(grad_packed, me, size).T
+    vector_sum = reduce_vector(grad_vector, me, size, zero_size)
     packed_new, packed_first_new, packed_second_new = adam_update(
         packed_weights, packed_first, packed_second, packed_sum
     )
@@ -258,8 +346,10 @@
 
 
 def solution(mesh):
+    zero_size = mesh.shape["zero"]
+    size = mesh.shape["dp"] * zero_size
     return jax.shard_map(
-        body,
+        functools.partial(body, zero_size, size),
         mesh=mesh,
         in_specs=(
             P(("dp", "zero"), None),

time: 585 us -> 391 us (0.67)
  waiting for transfers between devices: 356 us -> 173 us
  starting transfers between devices: 0.39 us -> 76.8 us
  blocking collectives: 77.7 us -> 4.54 us
  other arithmetic: 27.7 us -> 47.6 us
  matrix products: 63.9 us -> 44.9 us
  between operations: 14.5 us -> 2.51 us
  local copies, waits for them, and re-layouts: 42.8 us -> 35.2 us
    ppermute x0 -> x53, waiting for transfers between devices: none -> 173 us  [exchange(): return lax.ppermute(value, AXES, [(i, i ^ mask) for i in range(size)])]
    reduce_scatter x2 -> x0, waiting for transfers between devices: 134 us -> none  [the longest x1 134 us: body(): lax.psum_scatter(grad_down, ('dp', 'zero'), scatter_dimension=0, tiled=True)]
    unnamed x6 -> x0, waiting for transfers between devices: 119 us -> none
    all_gather x2 -> x0, waiting for transfers between devices: 103 us -> none  [the longest x1 81.4 us: body(): lax.all_gather(packed_shard, ('dp', 'zero'), axis=1, tiled=True)]
    ppermute x0 -> x53, starting transfers between devices: none -> 76.8 us  [exchange(): return lax.ppermute(value, AXES, [(i, i ^ mask) for i in range(size)])]
    psum x1 -> x0, blocking collectives: 75.8 us -> none  [body(): vector_sum = lax.psum(vector_part, 'dp')]
    unnamed x108 -> x134, local copies, waits for them, and re-layouts: 33.3 us -> 8.03 us
    another operation x1 -> x33, other arithmetic: 0.05 us -> 15 us  [the longest x32 14.9 us: gather_rows(): value = jnp.stack(slots, axis=axis)]
  transfers between devices with their start and end apart: 5 -> 53, of which waited for: 4 -> 26; matrix products, arithmetic and copies ran while one was open for 14% -> 24% of each run, Pallas kernels for 0% -> 0%
where the time goes in v1:
time: 391 us; the launch traced here: 384 us
  waiting for transfers between devices  173 us (44%)
  starting transfers between devices  76.8 us (20%)
  other arithmetic  47.6 us (12%)
  matrix products  44.9 us (11%)
  local copies, waits for them, and re-layouts  35.2 us (9%)
  blocking collectives  4.54 us (1%)
    ppermute x53, waiting for transfers between devices, exchange(): return lax.ppermute(value, AXES, [(i, i ^ mask) for i in range(size)])  173 us
    ppermute x53, starting transfers between devices, exchange(): return lax.ppermute(value, AXES, [(i, i ^ mask) for i in range(size)])  76.8 us
    dot_general x6, matrix products, contract(): return jnp.einsum(form, left, right, preferred_element_type=jnp.float32)  16.4 us
    another operation x32, other arithmetic, gather_rows(): value = jnp.stack(slots, axis=axis)  14.9 us
    add x4, other arithmetic, scatter_parts(): value = keep + exchange(send, size, 1)  10.7 us
    unnamed x134, local copies, waits for them, and re-layouts  8.03 us
  transfers between devices with their start and end apart: 53, of which 26 were waited for; matrix products, arithmetic and copies ran while one was open for 24% of the time, Pallas kernels for 0%

profile of v1, /device:TPU:0, one launch (start us, length us, event | category | flops | bytes accessed | tf_op | source)
XLA Modules:
  0.0 384.4 jit_solution(11656091040379098398)
XLA Ops:
  1.8 5.1 %collective-permute-start = (bf16[192,384]{1,0:T(8,128)(2,1)S(1)}, bf16[192,384]{1,0:T(8,128)(2,1)S(1)}, u32[]{:S(2)}, u32[]{:S(2)}) collective-permute-start(bf16[192,384]{1,0:T(8,128)(2,1)S(1)} %slice.159), channel_id=1, source_target_pairs={{0,24},{1,25},{2,26},{3,27},{4,28},{5,29},{6,30},{7,31},{8,16},{9,... | collective-permute-start | bytes 442376 | tf_op jit(solution)/shard_map/ppermute | solution.py:208
  7.5 4.1 %collective-permute-done = bf16[192,384]{1,0:T(8,128)(2,1)S(1)} collective-permute-done((bf16[192,384]{1,0:T(8,128)(2,1)S(1)}, bf16[192,384]{1,0:T(8,128)(2,1)S(1)}, u32[]{:S(2)}, u32[]{:S(2)}) %collective-permute-start) | collective-permute-done | bytes 147488 | tf_op jit(solution)/shard_map/ppermute | solution.py:208
  11.7 7.7 %collective-permute-done.1 = bf16[192,384]{1,0:T(8,128)(2,1)S(1)} collective-permute-done((bf16[192,384]{1,0:T(8,128)(2,1)S(1)}, bf16[192,384]{1,0:T(8,128)(2,1)S(1)}, u32[]{:S(2)}, u32[]{:S(2)}) %collective-permute-start.1) | collective-permute-done | bytes 147488 | tf_op jit(solution)/shard_map/ppermute | solution.py:208
  25.5 4.2 %collective-permute-done.6 = bf16[192,384]{1,0:T(8,128)(2,1)S(1)} collective-permute-done((bf16[192,384]{1,0:T(8,128)(2,1)S(1)}, bf16[192,384]{1,0:T(8,128)(2,1)S(1)}, u32[]{:S(2)}, u32[]{:S(2)}) %collective-permute-start.6) | collective-permute-done | bytes 147488 | tf_op jit(solution)/shard_map/ppermute | solution.py:208
  29.7 5.2 %collective-permute-done.7 = bf16[192,384]{1,0:T(8,128)(2,1)S(1)} collective-permute-done((bf16[192,384]{1,0:T(8,128)(2,1)S(1)}, bf16[192,384]{1,0:T(8,128)(2,1)S(1)}, u32[]{:S(2)}, u32[]{:S(2)}) %collective-permute-start.7) | collective-permute-done | bytes 147488 | tf_op jit(solution)/shard_map/ppermute | solution.py:208
  39.3 12.2 %collective-permute-done.9 = bf16[2,2,192,384]{3,2,1,0:T(8,128)(2,1)} collective-permute-done((bf16[2,2,192,384]{3,2,1,0:T(8,128)(2,1)S(1)}, bf16[2,2,192,384]{3,2,1,0:T(8,128)(2,1)}, u32[]{:S(2)}, u32[]{:S(2)}) %collective-permute-start.9) | collective-permute-done | bytes 589856 | tf_op jit(solution)/shard_map/ppermute | solution.py:208
  54.4 20.6 %collective-permute-done.4 = bf16[2,2,2,192,384]{4,3,2,1,0:T(8,128)(2,1)} collective-permute-done((bf16[2,2,2,192,384]{4,3,2,1,0:T(8,128)(2,1)}, bf16[2,2,2,192,384]{4,3,2,1,0:T(8,128)(2,1)}, u32[]{:S(2)}, u32[]{:S(2)}) %collective-permute-start.4) | collective-permute-done | bytes 1179680 | tf_op jit(solution)/shard_map/ppermute | solution.py:208
  78.3 4.5 %all_gather.3 = bf16[13,768]{1,0:T(8,128)(2,1)S(1)} all-gather(bf16[13,384]{1,0:T(8,128)(2,1)S(1)} %convert_element_type.144), channel_id=1, replica_groups=mesh['dp'=16,'zero'=2] {'zero'}, dimensions={1}, use_global_device_ids=true | all-gather | bytes 29952 | tf_op jit(solution)/shard_map/all_gather | solution.py:314
  124.1 5.2 %multiply_reduce_fusion = (f32[256,12]{0,1:T(8,128)S(1)}, bf16[256,12,64]{0,2,1:T(8,128)(2,1)}) fusion(bf16[256,12,64]{0,2,1:T(8,128)(2,1)S(1)} %bitcast.344, bf16[256,12,64]{0,2,1:T(8,128)(2,1)S(1)} %bitcast.338, f32[12,256,256]{1,2,0:T(8,128)} %fusion.100, pred[256,256]{0,1:T(8,128)(4,1)S(1)} %compare_and_fusion), kind=kOutput, calls=%fused_computation.130 | convolution fusion | flops 106168576 | bytes 4403200 | tf_op jit(solution)/shard_map/hqk,khd->qhd/dot_general | solution.py:27
  134.9 5.3 %fusion.52 = f32[12,64,256]{2,1,0:T(8,128)} fusion(bf16[256,12,64]{0,2,1:T(8,128)(2,1)S(1)} %bitcast.346, f32[12,256,256]{1,2,0:T(8,128)} %fusion.100, pred[256,256]{0,1:T(8,128)(4,1)S(1)} %compare_and_fusion), kind=kOutput, calls=%fused_computation.131 | convolution fusion | flops 105385216 | bytes 4390912 | tf_op jit(solution)/shard_map/hqk,qhd->khd/dot_general | solution.py:27
  148.8 10.2 %collective-permute-done.43 = bf16[2,2,2,96,384]{4,3,2,1,0:T(8,128)(2,1)S(1)} collective-permute-done((bf16[2,2,2,96,384]{4,3,2,1,0:T(8,128)(2,1)S(1)}, bf16[2,2,2,96,384]{4,3,2,1,0:T(8,128)(2,1)S(1)}, u32[]{:S(2)}, u32[]{:S(2)}) %collective-permute-start.43) | collective-permute-done | bytes 589856 | tf_op jit(solution)/shard_map/ppermute | solution.py:208
  163.9 4.0 %collective-permute-done.44 = bf16[2,2,96,384]{3,2,1,0:T(8,128)(2,1)S(1)} collective-permute-done((bf16[2,2,96,384]{3,2,1,0:T(8,128)(2,1)S(1)}, bf16[2,2,96,384]{3,2,1,0:T(8,128)(2,1)S(1)}, u32[]{:S(2)}, u32[]{:S(2)}) %collective-permute-start.44) | collective-permute-done | bytes 294944 | tf_op jit(solution)/shard_map/ppermute | solution.py:208
  178.7 8.9 %collective-permute-done.46 = f32[96,384]{1,0:T(8,128)S(1)} collective-permute-done((f32[96,384]{1,0:T(8,128)S(1)}, f32[96,384]{1,0:T(8,128)S(1)}, u32[]{:S(2)}, u32[]{:S(2)}) %collective-permute-start.46) | collective-permute-done | bytes 147488 | tf_op jit(solution)/shard_map/ppermute | solution.py:208
  187.7 6.6 %collective-permute-done.40 = f32[96,384]{1,0:T(8,128)S(1)} collective-permute-done((f32[96,384]{1,0:T(8,128)S(1)}, f32[96,384]{1,0:T(8,128)S(1)}, u32[]{:S(2)}, u32[]{:S(2)}) %collective-permute-start.40) | collective-permute-done | bytes 147488 | tf_op jit(solution)/shard_map/ppermute | solution.py:208
  218.6 4.9 %collective-permute-done.21 = bf16[2,2,96,384]{3,2,1,0:T(8,128)(2,1)S(1)} collective-permute-done((bf16[2,2,96,384]{3,2,1,0:T(8,128)(2,1)S(1)}, bf16[2,2,96,384]{3,2,1,0:T(8,128)(2,1)S(1)}, u32[]{:S(2)}, u32[]{:S(2)}) %collective-permute-start.21) | collective-permute-done | bytes 294944 | tf_op jit(solution)/shard_map/ppermute | solution.py:208
  226.9 8.4 %collective-permute-done.16 = bf16[2,2,2,96,384]{4,3,2,1,0:T(8,128)(2,1)S(1)} collective-permute-done((bf16[2,2,2,96,384]{4,3,2,1,0:T(8,128)(2,1)S(1)}, bf16[2,2,2,96,384]{4,3,2,1,0:T(8,128)(2,1)S(1)}, u32[]{:S(2)}, u32[]{:S(2)}) %collective-permute-start.16) | collective-permute-done | bytes 589856 | tf_op jit(solution)/shard_map/ppermute | solution.py:208
  260.0 4.4 %fusion.50 = f32[256,768]{1,0:T(8,128)S(1)} fusion(bf16[256,3072]{1,0:T(8,128)(2,1)} %copy-done.42, bf16[6144,384]{1,0:T(8,128)(2,1)} %bitcast.293, bf16[6144,384]{1,0:T(8,128)(2,1)} %bitcast.289), kind=kOutput, calls=%fused_computation.128 | convolution fusion | flops 1217396736 | bytes 11796480 | tf_op jit(solution)/shard_map/dot_general | solution.py:135
  284.5 23.0 %collective-permute-done.49 = f32[13,768]{1,0:T(8,128)S(1)} collective-permute-done((f32[13,768]{1,0:T(8,128)S(1)}, f32[13,768]{1,0:T(8,128)S(1)}, u32[]{:S(2)}, u32[]{:S(2)}) %collective-permute-start.49) | collective-permute-done | bytes 39968 | tf_op jit(solution)/shard_map/ppermute | solution.py:208
  309.1 3.9 %fusion.19 = f32[256,768]{1,0:T(8,128)S(1)} fusion(bf16[256,3072]{1,0:T(8,128)(2,1)S(1)} %copy-done.34, bf16[3072,384]{1,0:T(8,128)(2,1)} %bitcast.327, bf16[3072,384]{1,0:T(8,128)(2,1)} %bitcast.325, f32[768]{0:T(1024)S(1)} %get-tuple-element.27), kind=kOutput, calls=%fused_computation.68 | convolution fusion | flops 1217593344 | bytes 7080960 | tf_op jit(solution)/shard_map/dot_general | solution.py:124
  322.5 7.1 %collective-permute-done.32 = bf16[2,2,192,384]{3,2,1,0:T(8,128)(2,1)S(1)} collective-permute-done((bf16[2,2,192,384]{3,2,1,0:T(8,128)(2,1)S(1)}, bf16[2,2,192,384]{3,2,1,0:T(8,128)(2,1)S(1)}, u32[]{:S(2)}, u32[]{:S(2)}) %collective-permute-start.32) | collective-permute-done | bytes 589856 | tf_op jit(solution)/shard_map/ppermute | solution.py:208
  336.7 5.0 %collective-permute-done.35 = f32[192,384]{1,0:T(8,128)S(1)} collective-permute-done((f32[192,384]{1,0:T(8,128)S(1)}, f32[192,384]{1,0:T(8,128)S(1)}, u32[]{:S(2)}, u32[]{:S(2)}) %collective-permute-start.35) | collective-permute-done | bytes 294944 | tf_op jit(solution)/shard_map/ppermute | solution.py:208
  341.7 13.2 %collective-permute-start.27 = (f32[192,384]{1,0:T(8,128)S(1)}, f32[192,384]{1,0:T(8,128)S(1)}, u32[]{:S(2)}, u32[]{:S(2)}) collective-permute-start(f32[192,384]{1,0:T(8,128)S(1)} %get-tuple-element.74), channel_id=1, source_target_pairs={{0,8},{1,9},{2,10},{3,11},{4,12},{5,13},{6,14},{7,15},{8,0},{9,1},... | collective-permute-start | bytes 884744 | tf_op jit(solution)/shard_map/ppermute | solution.py:208
  355.6 15.2 %collective-permute-done.34 = f32[192,384]{1,0:T(8,128)S(1)} collective-permute-done((f32[192,384]{1,0:T(8,128)S(1)}, f32[192,384]{1,0:T(8,128)S(1)}, u32[]{:S(2)}, u32[]{:S(2)}) %collective-permute-start.34) | collective-permute-done | bytes 294944 | tf_op jit(solution)/shard_map/ppermute | solution.py:208
  370.9 11.3 %collective-permute-done.28 = f32[192,384]{1,0:T(8,128)S(1)} collective-permute-done((f32[192,384]{1,0:T(8,128)S(1)}, f32[192,384]{1,0:T(8,128)S(1)}, u32[]{:S(2)}, u32[]{:S(2)}) %collective-permute-start.28) | collective-permute-done | bytes 294944 | tf_op jit(solution)/shard_map/ppermute | solution.py:208
  (364 shorter events, 181.4 us)
Async XLA Ops:
  19.6 17.1 %collective-permute-start.3 = (bf16[2,2,192,384]{3,2,1,0:T(8,128)(2,1)S(1)}, bf16[2,2,192,384]{3,2,1,0:T(8,128)(2,1)S(1)}, u32[]{:S(2)}, u32[]{:S(2)}) collective-permute-start(bf16[2,2,192,384]{3,2,1,0:T(8,128)(2,1)S(1)} %bitcast.320), channel_id=1, source_target_pairs={{0,4},{1,5},{2,6},{3,7},{4,0},{5,1},{6,2},{7,3},{8,12},{9,13},{10,... | collective-permute-start | bytes 1769480 | tf_op jit(solution)/shard_map/ppermute | solution.py:208
  35.1 16.4 %collective-permute-start.9 = (bf16[2,2,192,384]{3,2,1,0:T(8,128)(2,1)S(1)}, bf16[2,2,192,384]{3,2,1,0:T(8,128)(2,1)}, u32[]{:S(2)}, u32[]{:S(2)}) collective-permute-start(bf16[2,2,192,384]{3,2,1,0:T(8,128)(2,1)S(1)} %bitcast.322), channel_id=1, source_target_pairs={{0,2},{1,3},{2,0},{3,1},{4,6},{5,7},{6,4},{7,5},{8,10},{9,11},{10,... | collective-permute-start | bytes 1769480 | tf_op jit(solution)/shard_map/ppermute | solution.py:208
  38.8 36.3 %collective-permute-start.4 = (bf16[2,2,2,192,384]{4,3,2,1,0:T(8,128)(2,1)}, bf16[2,2,2,192,384]{4,3,2,1,0:T(8,128)(2,1)}, u32[]{:S(2)}, u32[]{:S(2)}) collective-permute-start(bf16[2,2,2,192,384]{4,3,2,1,0:T(8,128)(2,1)} %pad_maximum_fusion.15), channel_id=1, source_target_pairs={{0,2},{1,3},{2,0},{3,1},{4,6},{5,7},{6,4},{7,5},{8,10},{9,11},{10,... | collective-permute-start | bytes 3538952 | tf_op jit(solution)/shard_map/ppermute | solution.py:208
  53.9 32.9 %collective-permute-start.10 = (bf16[2,2,2,192,384]{4,3,2,1,0:T(8,128)(2,1)}, bf16[2,2,2,192,384]{4,3,2,1,0:T(8,128)(2,1)}, u32[]{:S(2)}, u32[]{:S(2)}) collective-permute-start(bf16[2,2,2,192,384]{4,3,2,1,0:T(8,128)(2,1)} %pad_maximum_fusion.16), channel_id=1, source_target_pairs={{0,4},{1,5},{2,6},{3,7},{4,0},{5,1},{6,2},{7,3},{8,12},{9,13},{10,... | collective-permute-start | bytes 3538952 | tf_op jit(solution)/shard_map/ppermute | solution.py:208
  106.6 33.6 %collective-permute-start.42 = (f32[16,96,384]{2,1,0:T(8,128)}, f32[16,96,384]{2,1,0:T(8,128)}, u32[]{:S(2)}, u32[]{:S(2)}) collective-permute-start(f32[16,96,384]{2,1,0:T(8,128)} %dynamic-slice_bitcast_fusion), channel_id=1, source_target_pairs={{0,1},{1,0},{2,3},{3,2},{4,5},{5,4},{6,7},{7,6},{8,9},{9,8},{10,11... | collective-permute-start | bytes 7077896 | tf_op jit(solution)/shard_map/ppermute | solution.py:208
  109.4 34.5 %collective-permute-start.36 = (f32[16,96,384]{2,1,0:T(8,128)}, f32[16,96,384]{2,1,0:T(8,128)}, u32[]{:S(2)}, u32[]{:S(2)}) collective-permute-start(f32[16,96,384]{2,1,0:T(8,128)} %dynamic-slice_bitcast_fusion.1), channel_id=1, source_target_pairs={{0,1},{1,0},{2,3},{3,2},{4,5},{5,4},{6,7},{7,6},{8,9},{9,8},{10,11... | collective-permute-start | bytes 7077896 | tf_op jit(solution)/shard_map/ppermute | solution.py:208
  143.3 15.6 %collective-permute-start.43 = (bf16[2,2,2,96,384]{4,3,2,1,0:T(8,128)(2,1)S(1)}, bf16[2,2,2,96,384]{4,3,2,1,0:T(8,128)(2,1)S(1)}, u32[]{:S(2)}, u32[]{:S(2)}) collective-permute-start(bf16[2,2,2,96,384]{4,3,2,1,0:T(8,128)(2,1)S(1)} %fusion.67), channel_id=1, source_target_pairs={{0,4},{1,5},{2,6},{3,7},{4,0},{5,1},{6,2},{7,3},{8,12},{9,13},{10,... | collective-permute-start | bytes 1769480 | tf_op jit(solution)/shard_map/ppermute | solution.py:208
  146.0 15.8 %collective-permute-start.37 = (bf16[2,2,2,96,384]{4,3,2,1,0:T(8,128)(2,1)S(1)}, bf16[2,2,2,96,384]{4,3,2,1,0:T(8,128)(2,1)S(1)}, u32[]{:S(2)}, u32[]{:S(2)}) collective-permute-start(bf16[2,2,2,96,384]{4,3,2,1,0:T(8,128)(2,1)S(1)} %fusion.66), channel_id=1, source_target_pairs={{0,2},{1,3},{2,0},{3,1},{4,6},{5,7},{6,4},{7,5},{8,10},{9,11},{10,... | collective-permute-start | bytes 1769480 | tf_op jit(solution)/shard_map/ppermute | solution.py:208
  170.4 17.2 %collective-permute-start.46 = (f32[96,384]{1,0:T(8,128)S(1)}, f32[96,384]{1,0:T(8,128)S(1)}, u32[]{:S(2)}, u32[]{:S(2)}) collective-permute-start(f32[96,384]{1,0:T(8,128)S(1)} %get-tuple-element.115), channel_id=1, source_target_pairs={{0,16},{1,17},{2,18},{3,19},{4,20},{5,21},{6,22},{7,23},{8,24},{9,... | collective-permute-start | bytes 442376 | tf_op jit(solution)/shard_map/ppermute | solution.py:208
  170.4 17.2 %collective-permute-start.45 = (f32[96,384]{1,0:T(8,128)S(1)}, f32[96,384]{1,0:T(8,128)S(1)}, u32[]{:S(2)}, u32[]{:S(2)}) collective-permute-start(f32[96,384]{1,0:T(8,128)S(1)} %get-tuple-element.113), channel_id=1, source_target_pairs={{0,8},{1,9},{2,10},{3,11},{4,12},{5,13},{6,14},{7,15},{8,0},{9,1},... | collective-permute-start | bytes 442376 | tf_op jit(solution)/shard_map/ppermute | solution.py:208
  172.7 15.0 %collective-permute-start.41 = (f32[96,384]{1,0:T(8,128)S(1)}, f32[96,384]{1,0:T(8,128)S(1)}, u32[]{:S(2)}, u32[]{:S(2)}) collective-permute-start(f32[96,384]{1,0:T(8,128)S(1)} %get-tuple-element.111), channel_id=1, source_target_pairs={{0,24},{1,25},{2,26},{3,27},{4,28},{5,29},{6,30},{7,31},{8,16},{9,... | collective-permute-start | bytes 442376 | tf_op jit(solution)/shard_map/ppermute | solution.py:208
  175.0 19.3 %collective-permute-start.40 = (f32[96,384]{1,0:T(8,128)S(1)}, f32[96,384]{1,0:T(8,128)S(1)}, u32[]{:S(2)}, u32[]{:S(2)}) collective-permute-start(f32[96,384]{1,0:T(8,128)S(1)} %get-tuple-element.112), channel_id=1, source_target_pairs={{0,16},{1,17},{2,18},{3,19},{4,20},{5,21},{6,22},{7,23},{8,24},{9,... | collective-permute-start | bytes 442376 | tf_op jit(solution)/shard_map/ppermute | solution.py:208
  176.8 17.5 %collective-permute-start.39 = (f32[96,384]{1,0:T(8,128)S(1)}, f32[96,384]{1,0:T(8,128)S(1)}, u32[]{:S(2)}, u32[]{:S(2)}) collective-permute-start(f32[96,384]{1,0:T(8,128)S(1)} %get-tuple-element.110), channel_id=1, source_target_pairs={{0,8},{1,9},{2,10},{3,11},{4,12},{5,13},{6,14},{7,15},{8,0},{9,1},... | collective-permute-start | bytes 442376 | tf_op jit(solution)/shard_map/ppermute | solution.py:208
  217.1 18.2 %collective-permute-start.16 = (bf16[2,2,2,96,384]{4,3,2,1,0:T(8,128)(2,1)S(1)}, bf16[2,2,2,96,384]{4,3,2,1,0:T(8,128)(2,1)S(1)}, u32[]{:S(2)}, u32[]{:S(2)}) collective-permute-start(bf16[2,2,2,96,384]{4,3,2,1,0:T(8,128)(2,1)S(1)} %pad_maximum_fusion.25), channel_id=1, source_target_pairs={{0,2},{1,3},{2,0},{3,1},{4,6},{5,7},{6,4},{7,5},{8,10},{9,11},{10,... | collective-permute-start | bytes 1769480 | tf_op jit(solution)/shard_map/ppermute | solution.py:208
  271.5 41.6 %collective-permute-start.31 = (bf16[2,2,2,192,384]{4,3,2,1,0:T(8,128)(2,1)}, bf16[2,2,2,192,384]{4,3,2,1,0:T(8,128)(2,1)}, u32[]{:S(2)}, u32[]{:S(2)}) collective-permute-start(bf16[2,2,2,192,384]{4,3,2,1,0:T(8,128)(2,1)} %fusion.23), channel_id=1, source_target_pairs={{0,4},{1,5},{2,6},{3,7},{4,0},{5,1},{6,2},{7,3},{8,12},{9,13},{10,... | collective-permute-start | bytes 3538952 | tf_op jit(solution)/shard_map/ppermute | solution.py:208
  277.9 38.6 %collective-permute-start.25 = (bf16[2,2,2,192,384]{4,3,2,1,0:T(8,128)(2,1)}, bf16[2,2,2,192,384]{4,3,2,1,0:T(8,128)(2,1)}, u32[]{:S(2)}, u32[]{:S(2)}) collective-permute-start(bf16[2,2,2,192,384]{4,3,2,1,0:T(8,128)(2,1)} %fusion.22), channel_id=1, source_target_pairs={{0,2},{1,3},{2,0},{3,1},{4,6},{5,7},{6,4},{7,5},{8,10},{9,11},{10,... | collective-permute-start | bytes 3538952 | tf_op jit(solution)/shard_map/ppermute | solution.py:208
  282.9 24.6 %collective-permute-start.49 = (f32[13,768]{1,0:T(8,128)S(1)}, f32[13,768]{1,0:T(8,128)S(1)}, u32[]{:S(2)}, u32[]{:S(2)}) collective-permute-start(f32[13,768]{1,0:T(8,128)S(1)} %add.381), channel_id=1, source_target_pairs={{0,2},{1,3},{2,0},{3,1},{4,6},{5,7},{6,4},{7,5},{8,10},{9,11},{10,... | collective-permute-start | bytes 119816 | tf_op jit(solution)/shard_map/ppermute | solution.py:208
  318.1 16.2 %collective-permute-start.26 = (bf16[2,2,192,384]{3,2,1,0:T(8,128)(2,1)S(1)}, bf16[2,2,192,384]{3,2,1,0:T(8,128)(2,1)S(1)}, u32[]{:S(2)}, u32[]{:S(2)}) collective-permute-start(bf16[2,2,192,384]{3,2,1,0:T(8,128)(2,1)S(1)} %fusion.64), channel_id=1, source_target_pairs={{0,4},{1,5},{2,6},{3,7},{4,0},{5,1},{6,2},{7,3},{8,12},{9,13},{10,... | collective-permute-start | bytes 1769480 | tf_op jit(solution)/shard_map/ppermute | solution.py:208
  320.0 16.6 %collective-permute-start.52 = (f32[13,768]{1,0:T(8,128)S(1)}, f32[13,768]{1,0:T(8,128)S(1)}, u32[]{:S(2)}, u32[]{:S(2)}) collective-permute-start(f32[13,768]{1,0:T(8,128)S(1)} %add.384), channel_id=1, source_target_pairs={{0,16},{1,17},{2,18},{3,19},{4,20},{5,21},{6,22},{7,23},{8,24},{9,... | collective-permute-start | bytes 119816 | tf_op jit(solution)/shard_map/ppermute | solution.py:208
  331.9 39.0 %collective-permute-start.34 = (f32[192,384]{1,0:T(8,128)S(1)}, f32[192,384]{1,0:T(8,128)S(1)}, u32[]{:S(2)}, u32[]{:S(2)}) collective-permute-start(f32[192,384]{1,0:T(8,128)S(1)} %get-tuple-element.81), channel_id=1, source_target_pairs={{0,16},{1,17},{2,18},{3,19},{4,20},{5,21},{6,22},{7,23},{8,24},{9,... | collective-permute-start | bytes 884744 | tf_op jit(solution)/shard_map/ppermute | solution.py:208
  332.9 38.0 %collective-permute-start.33 = (f32[192,384]{1,0:T(8,128)S(1)}, f32[192,384]{1,0:T(8,128)S(1)}, u32[]{:S(2)}, u32[]{:S(2)}) collective-permute-start(f32[192,384]{1,0:T(8,128)S(1)} %get-tuple-element.79), channel_id=1, source_target_pairs={{0,8},{1,9},{2,10},{3,11},{4,12},{5,13},{6,14},{7,15},{8,0},{9,1},... | collective-permute-start | bytes 884744 | tf_op jit(solution)/shard_map/ppermute | solution.py:208
  334.5 36.4 %collective-permute-start.29 = (f32[192,384]{1,0:T(8,128)S(1)}, f32[192,384]{1,0:T(8,128)S(1)}, u32[]{:S(2)}, u32[]{:S(2)}) collective-permute-start(f32[192,384]{1,0:T(8,128)S(1)} %get-tuple-element.75), channel_id=1, source_target_pairs={{0,24},{1,25},{2,26},{3,27},{4,28},{5,29},{6,30},{7,31},{8,16},{9,... | collective-permute-start | bytes 884744 | tf_op jit(solution)/shard_map/ppermute | solution.py:208
  336.6 45.7 %collective-permute-start.28 = (f32[192,384]{1,0:T(8,128)S(1)}, f32[192,384]{1,0:T(8,128)S(1)}, u32[]{:S(2)}, u32[]{:S(2)}) collective-permute-start(f32[192,384]{1,0:T(8,128)S(1)} %get-tuple-element.76), channel_id=1, source_target_pairs={{0,16},{1,17},{2,18},{3,19},{4,20},{5,21},{6,22},{7,23},{8,24},{9,... | collective-permute-start | bytes 884744 | tf_op jit(solution)/shard_map/ppermute | solution.py:208
  341.7 40.5 %collective-permute-start.27 = (f32[192,384]{1,0:T(8,128)S(1)}, f32[192,384]{1,0:T(8,128)S(1)}, u32[]{:S(2)}, u32[]{:S(2)}) collective-permute-start(f32[192,384]{1,0:T(8,128)S(1)} %get-tuple-element.74), channel_id=1, source_target_pairs={{0,8},{1,9},{2,10},{3,11},{4,12},{5,13},{6,14},{7,15},{8,0},{9,1},... | collective-permute-start | bytes 884744 | tf_op jit(solution)/shard_map/ppermute | solution.py:208
  (96 other events, 906.6 us)

commit v2 on v1

--- a/solution.py
+++ b/solution.py
@@ -93,6 +93,18 @@
     weight_up = packed_low[4 * model_width :].T
     bias_qkv = vector_full[6:9].reshape(3 * model_width)
     bias_up = vector_full[9:].reshape(ffn_width)
+    upward = jnp.dot(normed_two_low, weight_up, preferred_element_type=jnp.float32) + bias_up
+    activated, gelu_slope = gelu_parts(upward)
+    activated_low = activated.astype(jnp.bfloat16)
+    grad_down = jnp.dot(activated_low.T, cotangent_rows, preferred_element_type=jnp.float32)
+    grad_upward = (
+        jnp.dot(cotangent_rows, down_low.T, preferred_element_type=jnp.float32) * gelu_slope
+    )
+    grad_upward_low = grad_upward.astype(jnp.bfloat16)
+    grad_weight_up = jnp.dot(grad_upward_low.T, normed_two_low, preferred_element_type=jnp.float32)
+    normed_one_low, grad_down, grad_weight_up = lax.optimization_barrier(
+        (normed_one_low, grad_down, grad_weight_up)
+    )
     projected = jnp.dot(normed_one_low, weight_qkv, preferred_element_type=jnp.float32) + bias_qkv
     heads_shape = (row_count, H, HEAD)
     cosine, sine_table, allowed = rotary_tables(segment_row)
@@ -117,21 +129,12 @@
     branch_attn = (
         jnp.dot(attended_low, weight_out, preferred_element_type=jnp.float32) + vector_full[4]
     )
-    upward = jnp.dot(normed_two_low, weight_up, preferred_element_type=jnp.float32) + bias_up
-    activated, gelu_slope = gelu_parts(upward)
-    activated_low = activated.astype(jnp.bfloat16)
     branch_mlp = (
         jnp.dot(activated_low, down_low, preferred_element_type=jnp.float32) + vector_full[5]
     )
     block_output = (residual + branch_attn + branch_mlp).astype(jnp.bfloat16)
     grad_rows = cotangent_rows.astype(jnp.float32)
     grad_bias_rows = jnp.sum(grad_rows, axis=0)
-    grad_down = jnp.dot(activated_low.T, cotangent_rows, preferred_element_type=jnp.float32)
-    grad_upward = (
-        jnp.dot(cotangent_rows, down_low.T, preferred_element_type=jnp.float32) * gelu_slope
-    )
-    grad_upward_low = grad_upward.astype(jnp.bfloat16)
-    grad_weight_up = jnp.dot(grad_upward_low.T, normed_two_low, preferred_element_type=jnp.float32)
     grad_normed_two = jnp.dot(grad_upward_low, weight_up.T, preferred_element_type=jnp.float32)
     grad_weight_out = jnp.dot(cotangent_rows.T, attended_low, preferred_element_type=jnp.float32)
     grad_attended_low = (
@@ -229,15 +232,16 @@
     return total, [b for b in present if b not in group]
 
 
-def scatter_parts(parts, me, size):
-    rows = sum(p.shape[0] for p in parts) // size
+def scatter_parts(parts, me, size, upper=None):
+    bit_count = size.bit_length() - 1
+    owners = bit_count if upper is None else bit_count - 1
+    rows = sum(p.shape[0] for p in parts) >> owners
     width = parts[0].shape[1]
-    bit_count = size.bit_length() - 1
     core = me & 1
     split = [p.reshape(p.shape[0] // (2 * rows), 2, rows, width) for p in parts]
     pieces = []
     half = width // 2
-    for index, stages in enumerate(stage_lists(bit_count)):
+    for index, first in enumerate(((1, 2), (2, 1))):
         cut = [p[..., index * half : (index + 1) * half] for p in split]
         send = jnp.concatenate(
             [lax.dynamic_index_in_dim(p, 1 - core, 1, keepdims=False) for p in cut], axis=0
@@ -246,16 +250,23 @@
             [lax.dynamic_index_in_dim(p, core, 1, keepdims=False) for p in cut], axis=0
         )
         value = keep + exchange(send, size, 1)
-        present = list(range(bit_count - 1, 0, -1))
-        value = value.reshape((2,) * (bit_count - 1) + (rows, half))
-        for group in stages:
-            wire = jnp.bfloat16 if group in ((1,), (2,)) else jnp.float32
-            value, present = scatter_stage(value, present, group, me, size, wire)
+        present = list(range(owners - 1, 0, -1))
+        value = value.reshape((2,) * (owners - 1) + (rows, half))
+        for b in first + tuple(range(3, owners)):
+            wire = jnp.bfloat16 if b in (1, 2) else jnp.float32
+            value, present = scatter_stage(value, present, (b,), me, size, wire)
+        if upper is not None:
+            middle = size // 2
+            if upper:
+                pairs = [(i, i + middle) for i in range(middle)]
+            else:
+                pairs = [(i + middle, i) for i in range(middle)]
+            value = value + lax.ppermute(value, AXES, pairs)
         pieces.append(value)
     return jnp.concatenate(pieces, axis=-1)
 
 
-def gather_rows(shard, me, size):
+def gather_rows(shard, cut_row, me, size):
     rows, width = shard.shape
     bit_count = size.bit_length() - 1
     half = width // 2
@@ -276,8 +287,12 @@
                 value.shape[:axis] + (2,) * len(group) + value.shape[axis + 1 :]
             )
             present = sorted(present + list(group), reverse=True)
-        pieces.append(value.reshape(size * rows, half))
-    return jnp.concatenate(pieces, axis=-1)
+        pieces.append(value.reshape(size, rows, half))
+    return jnp.concatenate(
+        [p[:, :cut_row].reshape(size * cut_row, half) for p in pieces], axis=-1
+    ), jnp.concatenate(
+        [p[:, cut_row:].reshape(size * (rows - cut_row), half) for p in pieces], axis=-1
+    )
 
 
 def reduce_vector(grad_vector, me, size, zero_size):
@@ -309,14 +324,17 @@
     packed_shard = packed_weights.astype(jnp.bfloat16).T
     down_shard = down_weights.astype(jnp.bfloat16)
     vector_shard = vector_params.astype(jnp.bfloat16)
-    packed_full = gather_rows(packed_shard, me, size)
-    down_full = gather_rows(down_shard, me, size)
+    packed_full, down_full = gather_rows(
+        jnp.concatenate([packed_shard, down_shard], axis=0), packed_shard.shape[0], me, size
+    )
     vector_full = lax.all_gather(vector_shard, "zero", axis=1, tiled=True)
     block_output, grad_tokens, grad_packed, grad_down, grad_vector = layer_rows(
         tokens, cotangent, segment_ids[0], packed_full, down_full, vector_full
     )
     down_sum = scatter_parts([grad_down], me, size)
-    packed_sum = scatter_parts(grad_packed, me, size).T
+    upper_sum = scatter_parts(grad_packed[2:], me, size, upper=True)
+    lower_sum = scatter_parts(grad_packed[:2], me, size, upper=False)
+    packed_sum = jnp.where(me >= size // 2, upper_sum, lower_sum).T
     vector_sum = reduce_vector(grad_vector, me, size, zero_size)
     packed_new, packed_first_new, packed_second_new = adam_update(
         packed_weights, packed_first, packed_second, packed_sum

time: 391 us -> 405 us (1.036)
  local copies, waits for them, and re-layouts: 35.2 us -> 53.2 us
  starting transfers between devices: 76.8 us -> 64.3 us
  other arithmetic: 47.6 us -> 53.1 us
    ppermute x53 -> x43, waiting for transfers between devices: 173 us -> 148 us  [exchange(): return lax.ppermute(value, AXES, [(i, i ^ mask) for i in range(size)])]
    ppermute x0 -> x4, waiting for transfers between devices: none -> 24.4 us  [scatter_parts(): value = value + lax.ppermute(value, AXES, pairs)]
    ppermute x53 -> x43, starting transfers between devices: 76.8 us -> 53.8 us  [exchange(): return lax.ppermute(value, AXES, [(i, i ^ mask) for i in range(size)])]
    slice x4, local copies, waits for them, and re-layouts: 3.46 us -> 16.1 us  [scatter_parts(): cut = [p[..., index * half:(index + 1) * half] for p in split]]
    ppermute x0 -> x4, starting transfers between devices: none -> 10.5 us  [scatter_parts(): value = value + lax.ppermute(value, AXES, pairs)]
    another operation x32 -> x16, other arithmetic: 14.9 us -> 24.7 us  [gather_rows(): value = jnp.stack(slots, axis=axis)]
    slice x2 -> x4, local copies, waits for them, and re-layouts: 0.03 us -> 8.11 us  [the longest x2 4.56 us: gather_rows(): p[:, :cut_row].reshape(size * cut_row, half)]
    squeeze x3, local copies, waits for them, and re-layouts: 7.39 us -> 0.64 us  [scatter_parts(): lax.dynamic_index_in_dim(p, core, 1, keepdims=False)]
  transfers between devices with their start and end apart: 53 -> 47, of which waited for: 26 -> 27; matrix products, arithmetic and copies ran while one was open for 24% -> 14% of each run, Pallas kernels for 0% -> 0%
where the time goes in v2:
time: 405 us; the launch traced here: 400 us
  waiting for transfers between devices  173 us (43%)
  starting transfers between devices  64.3 us (16%)
  local copies, waits for them, and re-layouts  53.2 us (13%)
  other arithmetic  53.1 us (13%)
  matrix products  47.5 us (12%)
  blocking collectives  6.68 us (2%)
    ppermute x43, waiting for transfers between devices, exchange(): return lax.ppermute(value, AXES, [(i, i ^ mask) for i in range(size)])  148 us
    ppermute x43, starting transfers between devices, exchange(): return lax.ppermute(value, AXES, [(i, i ^ mask) for i in range(size)])  53.8 us
    another operation x16, other arithmetic, gather_rows(): value = jnp.stack(slots, axis=axis)  24.7 us
    ppermute x4, waiting for transfers between devices, scatter_parts(): value = value + lax.ppermute(value, AXES, pairs)  24.4 us
    slice x4, local copies, waits for them, and re-layouts, scatter_parts(): cut = [p[..., index * half:(index + 1) * half] for p in split]  16.1 us
    dot_general x6, matrix products, contract(): return jnp.einsum(form, left, right, preferred_element_type=jnp.float32)  16 us
    ppermute x4, starting transfers between devices, scatter_parts(): value = value + lax.ppermute(value, AXES, pairs)  10.5 us
    add x6, other arithmetic, scatter_parts(): value = keep + exchange(send, size, 1)  9.02 us
  transfers between devices with their start and end apart: 47, of which 27 were waited for; matrix products, arithmetic and copies ran while one was open for 14% of the time, Pallas kernels for 0%

profile of v2, /device:TPU:0, one launch (start us, length us, event | category | flops | bytes accessed | tf_op | source)
XLA Modules:
  0.0 399.6 jit_solution(1146098589047834332)
XLA Ops:
  8.5 6.8 %collective-permute-done.2 = bf16[288,384]{1,0:T(8,128)(2,1)S(1)} collective-permute-done((bf16[288,384]{1,0:T(8,128)(2,1)S(1)}, bf16[288,384]{1,0:T(8,128)(2,1)S(1)}, u32[]{:S(2)}, u32[]{:S(2)}) %collective-permute-start.2) | collective-permute-done | bytes 221216 | tf_op jit(solution)/shard_map/ppermute | solution.py:211
  15.3 9.3 %collective-permute-done.1 = bf16[288,384]{1,0:T(8,128)(2,1)S(1)} collective-permute-done((bf16[288,384]{1,0:T(8,128)(2,1)S(1)}, bf16[288,384]{1,0:T(8,128)(2,1)S(1)}, u32[]{:S(2)}, u32[]{:S(2)}) %collective-permute-start.1) | collective-permute-done | bytes 221216 | tf_op jit(solution)/shard_map/ppermute | solution.py:211
  32.8 4.5 %collective-permute-done.8 = bf16[288,384]{1,0:T(8,128)(2,1)S(1)} collective-permute-done((bf16[288,384]{1,0:T(8,128)(2,1)S(1)}, bf16[288,384]{1,0:T(8,128)(2,1)S(1)}, u32[]{:S(2)}, u32[]{:S(2)}) %collective-permute-start.8) | collective-permute-done | bytes 221216 | tf_op jit(solution)/shard_map/ppermute | solution.py:211
  37.3 11.3 %collective-permute-done.7 = bf16[288,384]{1,0:T(8,128)(2,1)S(1)} collective-permute-done((bf16[288,384]{1,0:T(8,128)(2,1)S(1)}, bf16[288,384]{1,0:T(8,128)(2,1)S(1)}, u32[]{:S(2)}, u32[]{:S(2)}) %collective-permute-start.7) | collective-permute-done | bytes 221216 | tf_op jit(solution)/shard_map/ppermute | solution.py:211
  52.4 19.2 %collective-permute-done.9 = bf16[2,2,288,384]{3,2,1,0:T(8,128)(2,1)} collective-permute-done((bf16[2,2,288,384]{3,2,1,0:T(8,128)(2,1)S(1)}, bf16[2,2,288,384]{3,2,1,0:T(8,128)(2,1)}, u32[]{:S(2)}, u32[]{:S(2)}) %collective-permute-start.9) | collective-permute-done | bytes 884768 | tf_op jit(solution)/shard_map/ppermute | solution.py:211
  73.8 29.3 %collective-permute-done.4 = bf16[2,2,2,288,384]{4,3,2,1,0:T(8,128)(2,1)} collective-permute-done((bf16[2,2,2,288,384]{4,3,2,1,0:T(8,128)(2,1)S(1)}, bf16[2,2,2,288,384]{4,3,2,1,0:T(8,128)(2,1)}, u32[]{:S(2)}, u32[]{:S(2)}) %collective-permute-start.4) | collective-permute-done | bytes 1769504 | tf_op jit(solution)/shard_map/ppermute | solution.py:211
  111.9 6.7 %all_gather.3 = bf16[13,768]{1,0:T(8,128)(2,1)S(1)} all-gather(bf16[13,384]{1,0:T(8,128)(2,1)S(1)} %convert_element_type.180), channel_id=1, replica_groups=mesh['dp'=16,'zero'=2] {'zero'}, dimensions={1}, use_global_device_ids=true | all-gather | bytes 29952 | tf_op jit(solution)/shard_map/all_gather | solution.py:330
  141.0 4.8 %select_bitcast_fusion.1 = (bf16[2,2,2,2,1,288,384]{6,5,3,2,1,0,4:T(8,128)(2,1)}, bf16[2,2,2,2,1,288,384]{6,5,3,2,1,0,4:T(8,128)(2,1)}) fusion(bf16[2,2,2,2,288,384]{5,4,3,2,1,0:T(8,128)(2,1)} %collective-permute-done.11, pred[]{:T(512)S(6)} %eq.41, bf16[2,2,1,2,288,384]{5,4,3,2,1,0:T(8,128)(2,1)S(1)} %copy-done.7, ...), kind=kLoop, calls=%fused_computation.18 | loop fusion | flops 5308416 | bytes 14155777 | tf_op jit(solution)/shard_map/stack | solution.py:285
  168.0 5.3 %fusion.51 = f32[3072,768]{1,0:T(8,128)} fusion(bf16[256,3072]{1,0:T(8,128)(2,1)S(1)} %get-tuple-element.114, bf16[256,768]{1,0:T(8,128)(2,1)S(1)} %copy-done.8, f32[768]{0:T(1024)S(1)} %copy-done.52, f32[768]{0:T(1024)S(1)} %get-tuple-element.35, f32[256]{0:T(256)S(1)} %copy-done.54, f32[256]{0:T(256)S(1)} %copy-done.49), kind=kOutput, calls=%fused_computation.128 | convolution fusion | flops 1209139200 | bytes 11411456 | tf_op jit(solution)/shard_map/dot_general | solution.py:104
  173.3 5.0 %fusion.117 = f32[3072,768]{1,0:T(8,128)} fusion(bf16[256,3072]{1,0:T(8,128)(2,1)S(1)} %get-tuple-element.109, bf16[256,768]{1,0:T(8,128)(2,1)S(1)} %copy-done.19), kind=kOutput, calls=%fused_computation.265 | convolution fusion | flops 1207959552 | bytes 11403264 | tf_op jit(solution)/shard_map/dot_general | solution.py:99
  191.1 4.4 %fusion.46 = f32[12,64,256]{2,1,0:T(8,128)S(1)} fusion(bf16[256,12,64]{0,2,1:T(8,128)(2,1)S(1)} %bitcast.294, f32[12,256,256]{1,2,0:T(8,128)} %fusion.96, pred[256,256]{0,1:T(8,128)(4,1)S(1)} %copy-done.45), kind=kOutput, calls=%fused_computation.123 | convolution fusion | flops 105385216 | bytes 4390912 | tf_op jit(solution)/shard_map/hqk,qhd->khd/dot_general | solution.py:27
  195.6 5.5 %multiply_reduce_fusion = (f32[256,12]{0,1:T(8,128)S(1)}, bf16[256,12,64]{0,2,1:T(8,128)(2,1)}) fusion(bf16[256,12,64]{0,2,1:T(8,128)(2,1)S(1)} %bitcast.295, bf16[256,12,64]{0,2,1:T(8,128)(2,1)S(1)} %bitcast.292, f32[12,256,256]{1,2,0:T(8,128)} %fusion.96, pred[256,256]{0,1:T(8,128)(4,1)S(1)} %copy-done.45), kind=kOutput, calls=%fused_computation.122 | convolution fusion | flops 106168576 | bytes 4403200 | tf_op jit(solution)/shard_map/hqk,khd->qhd/dot_general | solution.py:27
  210.2 4.4 %fusion.109 = (f32[16,2,96,384]{3,2,1,0:T(8,128)S(1)}, f32[16,2,96,384]{3,2,1,0:T(8,128)S(1)}) fusion(f32[16,2,96,768]{3,2,1,0:T(8,128)} %bitcast.234), kind=kLoop, calls=%fused_computation.259 | loop fusion | bytes 18874368 | tf_op jit(solution)/shard_map/slice | solution.py:245
  214.6 7.7 %fusion.110 = (f32[8,2,192,384]{3,2,1,0:T(8,128)S(1)}, f32[8,2,192,384]{3,2,1,0:T(8,128)S(1)}) fusion(f32[8,2,192,768]{3,2,1,0:T(8,128)} %bitcast.235), kind=kLoop, calls=%fused_computation.260 | loop fusion | bytes 18874368 | tf_op jit(solution)/shard_map/slice | solution.py:245
  252.1 6.0 %collective-permute-start.45 = (f32[13,768]{1,0:T(8,128)S(1)}, f32[13,768]{1,0:T(8,128)S(1)}, u32[]{:S(2)}, u32[]{:S(2)}) collective-permute-start(f32[13,768]{1,0:T(8,128)S(1)} %add.415), channel_id=1, source_target_pairs={{0,8},{1,9},{2,10},{3,11},{4,12},{5,13},{6,14},{7,15},{8,0},{9,1},... | collective-permute-start | bytes 119816 | tf_op jit(solution)/shard_map/ppermute | solution.py:211
  291.7 7.8 %collective-permute-done.18 = bf16[2,2,192,384]{3,2,1,0:T(8,128)(2,1)S(1)} collective-permute-done((bf16[2,2,192,384]{3,2,1,0:T(8,128)(2,1)S(1)}, bf16[2,2,192,384]{3,2,1,0:T(8,128)(2,1)S(1)}, u32[]{:S(2)}, u32[]{:S(2)}) %collective-permute-start.18) | collective-permute-done | bytes 589856 | tf_op jit(solution)/shard_map/ppermute | solution.py:211
  304.4 7.8 %collective-permute-done.28 = bf16[2,2,192,384]{3,2,1,0:T(8,128)(2,1)S(1)} collective-permute-done((bf16[2,2,192,384]{3,2,1,0:T(8,128)(2,1)S(1)}, bf16[2,2,192,384]{3,2,1,0:T(8,128)(2,1)S(1)}, u32[]{:S(2)}, u32[]{:S(2)}) %collective-permute-start.28) | collective-permute-done | bytes 589856 | tf_op jit(solution)/shard_map/ppermute | solution.py:211
  317.0 4.7 %collective-permute-done.39 = bf16[2,2,96,384]{3,2,1,0:T(8,128)(2,1)S(1)} collective-permute-done((bf16[2,2,96,384]{3,2,1,0:T(8,128)(2,1)S(1)}, bf16[2,2,96,384]{3,2,1,0:T(8,128)(2,1)S(1)}, u32[]{:S(2)}, u32[]{:S(2)}) %collective-permute-start.39) | collective-permute-done | bytes 294944 | tf_op jit(solution)/shard_map/ppermute | solution.py:211
  341.2 8.0 %collective-permute-done.20 = f32[192,384]{1,0:T(8,128)S(1)} collective-permute-done((f32[192,384]{1,0:T(8,128)S(1)}, f32[192,384]{1,0:T(8,128)S(1)}, u32[]{:S(2)}, u32[]{:S(2)}) %collective-permute-start.20) | collective-permute-done | bytes 294944 | tf_op jit(solution)/shard_map/ppermute | solution.py:211
  349.5 7.6 %collective-permute-done.15 = f32[192,384]{1,0:T(8,128)S(1)} collective-permute-done((f32[192,384]{1,0:T(8,128)S(1)}, f32[192,384]{1,0:T(8,128)S(1)}, u32[]{:S(2)}, u32[]{:S(2)}) %collective-permute-start.15) | collective-permute-done | bytes 294944 | tf_op jit(solution)/shard_map/ppermute | solution.py:211
  363.5 5.8 %collective-permute-start.16 = (f32[192,384]{1,0:T(8,128)S(1)}, f32[192,384]{1,0:T(8,128)S(1)}, u32[]{:S(2)}, u32[]{:S(2)}) collective-permute-start(f32[192,384]{1,0:T(8,128)S(1)} %bitcast_add_fusion.21), channel_id=1, source_target_pairs={{0,16},{1,17},{2,18},{3,19},{4,20},{5,21},{6,22},{7,23},{8,24},{9,... | collective-permute-start | bytes 884744 | tf_op jit(solution)/shard_map/ppermute | solution.py:264
  374.9 4.4 %collective-permute-done.16 = f32[192,384]{1,0:T(8,128)S(1)} collective-permute-done((f32[192,384]{1,0:T(8,128)S(1)}, f32[192,384]{1,0:T(8,128)S(1)}, u32[]{:S(2)}, u32[]{:S(2)}) %collective-permute-start.16) | collective-permute-done | bytes 294944 | tf_op jit(solution)/shard_map/ppermute | solution.py:264
  379.3 14.1 %collective-permute-done.31 = f32[192,384]{1,0:T(8,128)S(1)} collective-permute-done((f32[192,384]{1,0:T(8,128)S(1)}, f32[192,384]{1,0:T(8,128)S(1)}, u32[]{:S(2)}, u32[]{:S(2)}) %collective-permute-start.31) | collective-permute-done | bytes 294944 | tf_op jit(solution)/shard_map/ppermute | solution.py:264
  393.5 4.2 %collective-permute-done.26 = f32[192,384]{1,0:T(8,128)S(1)} collective-permute-done((f32[192,384]{1,0:T(8,128)S(1)}, f32[192,384]{1,0:T(8,128)S(1)}, u32[]{:S(2)}, u32[]{:S(2)}) %collective-permute-start.26) | collective-permute-done | bytes 294944 | tf_op jit(solution)/shard_map/ppermute | solution.py:264
  (367 shorter events, 202.5 us)
Async XLA Ops:
  24.9 25.6 %collective-permute-start.3 = (bf16[2,2,288,384]{3,2,1,0:T(8,128)(2,1)S(1)}, bf16[2,2,288,384]{3,2,1,0:T(8,128)(2,1)S(1)}, u32[]{:S(2)}, u32[]{:S(2)}) collective-permute-start(bf16[2,2,288,384]{3,2,1,0:T(8,128)(2,1)S(1)} %bitcast.275), channel_id=1, source_target_pairs={{0,4},{1,5},{2,6},{3,7},{4,0},{5,1},{6,2},{7,3},{8,12},{9,13},{10,... | collective-permute-start | bytes 2654216 | tf_op jit(solution)/shard_map/ppermute | solution.py:211
  48.9 22.8 %collective-permute-start.9 = (bf16[2,2,288,384]{3,2,1,0:T(8,128)(2,1)S(1)}, bf16[2,2,288,384]{3,2,1,0:T(8,128)(2,1)}, u32[]{:S(2)}, u32[]{:S(2)}) collective-permute-start(bf16[2,2,288,384]{3,2,1,0:T(8,128)(2,1)S(1)} %bitcast.277), channel_id=1, source_target_pairs={{0,2},{1,3},{2,0},{3,1},{4,6},{5,7},{6,4},{7,5},{8,10},{9,11},{10,... | collective-permute-start | bytes 2654216 | tf_op jit(solution)/shard_map/ppermute | solution.py:211
  51.9 51.3 %collective-permute-start.4 = (bf16[2,2,2,288,384]{4,3,2,1,0:T(8,128)(2,1)S(1)}, bf16[2,2,2,288,384]{4,3,2,1,0:T(8,128)(2,1)}, u32[]{:S(2)}, u32[]{:S(2)}) collective-permute-start(bf16[2,2,2,288,384]{4,3,2,1,0:T(8,128)(2,1)S(1)} %pad_maximum_fusion.10), channel_id=1, source_target_pairs={{0,2},{1,3},{2,0},{3,1},{4,6},{5,7},{6,4},{7,5},{8,10},{9,11},{10,... | collective-permute-start | bytes 5308424 | tf_op jit(solution)/shard_map/ppermute | solution.py:211
  73.2 34.1 %collective-permute-start.10 = (bf16[2,2,2,288,384]{4,3,2,1,0:T(8,128)(2,1)S(1)}, bf16[2,2,2,288,384]{4,3,2,1,0:T(8,128)(2,1)S(1)}, u32[]{:S(2)}, u32[]{:S(2)}) collective-permute-start(bf16[2,2,2,288,384]{4,3,2,1,0:T(8,128)(2,1)S(1)} %pad_maximum_fusion.11), channel_id=1, source_target_pairs={{0,4},{1,5},{2,6},{3,7},{4,0},{5,1},{6,2},{7,3},{8,12},{9,13},{10,... | collective-permute-start | bytes 5308424 | tf_op jit(solution)/shard_map/ppermute | solution.py:211
  107.3 23.6 %collective-permute-start.5 = (bf16[2,2,2,2,288,384]{5,4,3,2,1,0:T(8,128)(2,1)}, bf16[2,2,2,2,288,384]{5,4,3,2,1,0:T(8,128)(2,1)}, u32[]{:S(2)}, u32[]{:S(2)}) collective-permute-start(bf16[2,2,2,2,288,384]{5,4,3,2,1,0:T(8,128)(2,1)} %pad_maximum_fusion.3), channel_id=1, source_target_pairs={{0,1},{1,0},{2,3},{3,2},{4,5},{5,4},{6,7},{7,6},{8,9},{9,8},{10,11... | collective-permute-start | bytes 10616840 | tf_op jit(solution)/shard_map/ppermute | solution.py:211
  110.6 29.3 %collective-permute-start.11 = (bf16[2,2,2,2,288,384]{5,4,3,2,1,0:T(8,128)(2,1)}, bf16[2,2,2,2,288,384]{5,4,3,2,1,0:T(8,128)(2,1)}, u32[]{:S(2)}, u32[]{:S(2)}) collective-permute-start(bf16[2,2,2,2,288,384]{5,4,3,2,1,0:T(8,128)(2,1)} %pad_maximum_fusion.4), channel_id=1, source_target_pairs={{0,1},{1,0},{2,3},{3,2},{4,5},{5,4},{6,7},{7,6},{8,9},{9,8},{10,11... | collective-permute-start | bytes 10616840 | tf_op jit(solution)/shard_map/ppermute | solution.py:211
  230.7 36.6 %collective-permute-start.37 = (f32[16,96,384]{2,1,0:T(8,128)}, f32[16,96,384]{2,1,0:T(8,128)}, u32[]{:S(2)}, u32[]{:S(2)}) collective-permute-start(f32[16,96,384]{2,1,0:T(8,128)} %dynamic-slice_bitcast_fusion), channel_id=1, source_target_pairs={{0,1},{1,0},{2,3},{3,2},{4,5},{5,4},{6,7},{7,6},{8,9},{9,8},{10,11... | collective-permute-start | bytes 7077896 | tf_op jit(solution)/shard_map/ppermute | solution.py:211
  231.0 39.7 %collective-permute-start.32 = (f32[16,96,384]{2,1,0:T(8,128)}, f32[16,96,384]{2,1,0:T(8,128)}, u32[]{:S(2)}, u32[]{:S(2)}) collective-permute-start(f32[16,96,384]{2,1,0:T(8,128)} %dynamic-slice_bitcast_fusion.1), channel_id=1, source_target_pairs={{0,1},{1,0},{2,3},{3,2},{4,5},{5,4},{6,7},{7,6},{8,9},{9,8},{10,11... | collective-permute-start | bytes 7077896 | tf_op jit(solution)/shard_map/ppermute | solution.py:211
  231.3 42.5 %collective-permute-start.17 = (f32[8,192,384]{2,1,0:T(8,128)}, f32[8,192,384]{2,1,0:T(8,128)}, u32[]{:S(2)}, u32[]{:S(2)}) collective-permute-start(f32[8,192,384]{2,1,0:T(8,128)} %dynamic-slice_bitcast_fusion.2), channel_id=1, source_target_pairs={{0,1},{1,0},{2,3},{3,2},{4,5},{5,4},{6,7},{7,6},{8,9},{9,8},{10,11... | collective-permute-start | bytes 7077896 | tf_op jit(solution)/shard_map/ppermute | solution.py:211
  231.5 46.0 %collective-permute-start.12 = (f32[8,192,384]{2,1,0:T(8,128)}, f32[8,192,384]{2,1,0:T(8,128)}, u32[]{:S(2)}, u32[]{:S(2)}) collective-permute-start(f32[8,192,384]{2,1,0:T(8,128)} %dynamic-slice_bitcast_fusion.3), channel_id=1, source_target_pairs={{0,1},{1,0},{2,3},{3,2},{4,5},{5,4},{6,7},{7,6},{8,9},{9,8},{10,11... | collective-permute-start | bytes 7077896 | tf_op jit(solution)/shard_map/ppermute | solution.py:211
  277.5 22.1 %collective-permute-start.18 = (bf16[2,2,192,384]{3,2,1,0:T(8,128)(2,1)S(1)}, bf16[2,2,192,384]{3,2,1,0:T(8,128)(2,1)S(1)}, u32[]{:S(2)}, u32[]{:S(2)}) collective-permute-start(bf16[2,2,192,384]{3,2,1,0:T(8,128)(2,1)S(1)} %fusion.63), channel_id=1, source_target_pairs={{0,4},{1,5},{2,6},{3,7},{4,0},{5,1},{6,2},{7,3},{8,12},{9,13},{10,... | collective-permute-start | bytes 1769480 | tf_op jit(solution)/shard_map/ppermute | solution.py:211
  281.0 21.8 %collective-permute-start.13 = (bf16[2,2,192,384]{3,2,1,0:T(8,128)(2,1)S(1)}, bf16[2,2,192,384]{3,2,1,0:T(8,128)(2,1)S(1)}, u32[]{:S(2)}, u32[]{:S(2)}) collective-permute-start(bf16[2,2,192,384]{3,2,1,0:T(8,128)(2,1)S(1)} %fusion.62), channel_id=1, source_target_pairs={{0,2},{1,3},{2,0},{3,1},{4,6},{5,7},{6,4},{7,5},{8,10},{9,11},{10,... | collective-permute-start | bytes 1769480 | tf_op jit(solution)/shard_map/ppermute | solution.py:211
  281.9 30.3 %collective-permute-start.28 = (bf16[2,2,192,384]{3,2,1,0:T(8,128)(2,1)S(1)}, bf16[2,2,192,384]{3,2,1,0:T(8,128)(2,1)S(1)}, u32[]{:S(2)}, u32[]{:S(2)}) collective-permute-start(bf16[2,2,192,384]{3,2,1,0:T(8,128)(2,1)S(1)} %fusion.65), channel_id=1, source_target_pairs={{0,4},{1,5},{2,6},{3,7},{4,0},{5,1},{6,2},{7,3},{8,12},{9,13},{10,... | collective-permute-start | bytes 1769480 | tf_op jit(solution)/shard_map/ppermute | solution.py:211
  286.9 28.4 %collective-permute-start.23 = (bf16[2,2,192,384]{3,2,1,0:T(8,128)(2,1)S(1)}, bf16[2,2,192,384]{3,2,1,0:T(8,128)(2,1)S(1)}, u32[]{:S(2)}, u32[]{:S(2)}) collective-permute-start(bf16[2,2,192,384]{3,2,1,0:T(8,128)(2,1)S(1)} %fusion.64), channel_id=1, source_target_pairs={{0,2},{1,3},{2,0},{3,1},{4,6},{5,7},{6,4},{7,5},{8,10},{9,11},{10,... | collective-permute-start | bytes 1769480 | tf_op jit(solution)/shard_map/ppermute | solution.py:211
  290.1 31.6 %collective-permute-start.39 = (bf16[2,2,96,384]{3,2,1,0:T(8,128)(2,1)S(1)}, bf16[2,2,96,384]{3,2,1,0:T(8,128)(2,1)S(1)}, u32[]{:S(2)}, u32[]{:S(2)}) collective-permute-start(bf16[2,2,96,384]{3,2,1,0:T(8,128)(2,1)S(1)} %fusion.75), channel_id=1, source_target_pairs={{0,2},{1,3},{2,0},{3,1},{4,6},{5,7},{6,4},{7,5},{8,10},{9,11},{10,... | collective-permute-start | bytes 884744 | tf_op jit(solution)/shard_map/ppermute | solution.py:211
  299.6 23.5 %collective-permute-start.34 = (bf16[2,2,96,384]{3,2,1,0:T(8,128)(2,1)S(1)}, bf16[2,2,96,384]{3,2,1,0:T(8,128)(2,1)S(1)}, u32[]{:S(2)}, u32[]{:S(2)}) collective-permute-start(bf16[2,2,96,384]{3,2,1,0:T(8,128)(2,1)S(1)} %fusion.74), channel_id=1, source_target_pairs={{0,4},{1,5},{2,6},{3,7},{4,0},{5,1},{6,2},{7,3},{8,12},{9,13},{10,... | collective-permute-start | bytes 884744 | tf_op jit(solution)/shard_map/ppermute | solution.py:211
  302.7 25.3 %collective-permute-start.19 = (bf16[2,192,384]{2,1,0:T(8,128)(2,1)S(1)}, bf16[2,192,384]{2,1,0:T(8,128)(2,1)S(1)}, u32[]{:S(2)}, u32[]{:S(2)}) collective-permute-start(bf16[2,192,384]{2,1,0:T(8,128)(2,1)S(1)} %fusion.71), channel_id=1, source_target_pairs={{0,2},{1,3},{2,0},{3,1},{4,6},{5,7},{6,4},{7,5},{8,10},{9,11},{10,... | collective-permute-start | bytes 884744 | tf_op jit(solution)/shard_map/ppermute | solution.py:211
  332.9 24.2 %collective-permute-start.15 = (f32[192,384]{1,0:T(8,128)S(1)}, f32[192,384]{1,0:T(8,128)S(1)}, u32[]{:S(2)}, u32[]{:S(2)}) collective-permute-start(f32[192,384]{1,0:T(8,128)S(1)} %dynamic-slice_bitcast_fusion.17), channel_id=1, source_target_pairs={{0,8},{1,9},{2,10},{3,11},{4,12},{5,13},{6,14},{7,15},{8,0},{9,1},... | collective-permute-start | bytes 884744 | tf_op jit(solution)/shard_map/ppermute | solution.py:211
  334.4 29.1 %collective-permute-start.30 = (f32[192,384]{1,0:T(8,128)S(1)}, f32[192,384]{1,0:T(8,128)S(1)}, u32[]{:S(2)}, u32[]{:S(2)}) collective-permute-start(f32[192,384]{1,0:T(8,128)S(1)} %dynamic-slice_bitcast_fusion.14), channel_id=1, source_target_pairs={{0,8},{1,9},{2,10},{3,11},{4,12},{5,13},{6,14},{7,15},{8,0},{9,1},... | collective-permute-start | bytes 884744 | tf_op jit(solution)/shard_map/ppermute | solution.py:211
  335.2 34.1 %collective-permute-start.25 = (f32[192,384]{1,0:T(8,128)S(1)}, f32[192,384]{1,0:T(8,128)S(1)}, u32[]{:S(2)}, u32[]{:S(2)}) collective-permute-start(f32[192,384]{1,0:T(8,128)S(1)} %dynamic-slice_bitcast_fusion.15), channel_id=1, source_target_pairs={{0,8},{1,9},{2,10},{3,11},{4,12},{5,13},{6,14},{7,15},{8,0},{9,1},... | collective-permute-start | bytes 884744 | tf_op jit(solution)/shard_map/ppermute | solution.py:211
  338.2 32.5 %collective-permute-start.41 = (f32[96,384]{1,0:T(8,128)S(1)}, f32[96,384]{1,0:T(8,128)S(1)}, u32[]{:S(2)}, u32[]{:S(2)}) collective-permute-start(f32[96,384]{1,0:T(8,128)S(1)} %dynamic-slice_bitcast_fusion.18), channel_id=1, source_target_pairs={{0,16},{1,17},{2,18},{3,19},{4,20},{5,21},{6,22},{7,23},{8,24},{9,... | collective-permute-start | bytes 442376 | tf_op jit(solution)/shard_map/ppermute | solution.py:211
  349.2 22.8 %collective-permute-start.36 = (f32[96,384]{1,0:T(8,128)S(1)}, f32[96,384]{1,0:T(8,128)S(1)}, u32[]{:S(2)}, u32[]{:S(2)}) collective-permute-start(f32[96,384]{1,0:T(8,128)S(1)} %dynamic-slice_bitcast_fusion.19), channel_id=1, source_target_pairs={{0,16},{1,17},{2,18},{3,19},{4,20},{5,21},{6,22},{7,23},{8,24},{9,... | collective-permute-start | bytes 442376 | tf_op jit(solution)/shard_map/ppermute | solution.py:211
  369.3 24.1 %collective-permute-start.31 = (f32[192,384]{1,0:T(8,128)S(1)}, f32[192,384]{1,0:T(8,128)S(1)}, u32[]{:S(2)}, u32[]{:S(2)}) collective-permute-start(f32[192,384]{1,0:T(8,128)S(1)} %bitcast_add_fusion.18), channel_id=1, source_target_pairs={{16,0},{17,1},{18,2},{19,3},{20,4},{21,5},{22,6},{23,7},{24,8},{25... | collective-permute-start | bytes 884744 | tf_op jit(solution)/shard_map/ppermute | solution.py:264
  370.7 27.0 %collective-permute-start.26 = (f32[192,384]{1,0:T(8,128)S(1)}, f32[192,384]{1,0:T(8,128)S(1)}, u32[]{:S(2)}, u32[]{:S(2)}) collective-permute-start(f32[192,384]{1,0:T(8,128)S(1)} %bitcast_add_fusion.19), channel_id=1, source_target_pairs={{16,0},{17,1},{18,2},{19,3},{20,4},{21,5},{22,6},{23,7},{24,8},{25... | collective-permute-start | bytes 884744 | tf_op jit(solution)/shard_map/ppermute | solution.py:264
  (90 other events, 807.1 us)
